TPU v7x, 32 devices: a whole 2x2x4 slice. The times are simulated.
32 devices in a mesh: groups: 2 (over y), seq: 4 (over z), head: 2 (over x), sub: 2 (over core).
Axes of the slice: x: 2, y: 2, z: 4, core: 2. Of those that a mesh axis runs over, the one named last changes fastest.
Arguments:
- queries: bfloat16 [8192, 2560], P(('groups', 'seq'), 'head'), parts along dimension 0, may hold values from -8 to 8
- cur_keys: bfloat16 [8192, 2560], P(('groups', 'seq', 'sub'), 'head'), parts along dimension 0, may hold values from -8 to 8
- cur_values: bfloat16 [8192, 2560], P(('groups', 'seq', 'sub'), 'head'), parts along dimension 0, may hold values from -6 to 6
- mem_keys: bfloat16 [256, 64, 2560], P(('groups', 'seq', 'sub'), None, 'head'), parts along dimension 0, may hold values from -6.5 to 6.5
- mem_values: bfloat16 [256, 64, 2560], P(('groups', 'seq', 'sub'), None, 'head'), parts along dimension 0, may hold values from -6 to 6
- frame_ids: int32 [8, 8], P('groups'), parts along dimension 0, may hold values from 0 to 127, as said below
- frame_counts: int32 [256], P('groups'), parts along dimension 0, may hold values from 1 to 64, as said below
- out_weight: bfloat16 [2560, 5120], P('head', 'sub'), may hold values from -0.125 to 0.125
Outputs:
- projected: bfloat16 [8192, 5120], P(('groups', 'seq', 'head'), 'sub'), parts along dimension 0
There are 2 independent parts, one for each index of `groups`. A program takes and returns all parts, laid end to end along the dimension named above; an argument that names none is the same for every part. Nothing has to cross between parts.
Inputs may be any that keep to these rules, and one draw needn't show every extreme that they name: `frame_ids`: row c lists the 8 memory frames retrieved for stretch c; frame f is held by owner f // 16, and the 8 frames of a row lie on 8 different owners, one on each. Frame f has its first frame_counts[f] token slots valid; the other slots are padding.
All inputs are finite; a program needn't handle non-finite values.
Results may differ from a plain program's by a relative error of at most 0.009.
Values may be sent and summed in bfloat16 or wider, within the bound.
No kernel may reach another device: no remote copies, remote signals or barrier semaphores. Data moves between devices by JAX's collectives and lax.ppermute only.
A program may use at most 192 MiB of HBM per device.

v0:
```python
import functools
import math

import jax
import jax.numpy as jnp
from jax import lax
from jax.experimental import pallas as pl
from jax.experimental.pallas import tpu as pltpu
from jax.sharding import PartitionSpec as P

HD = 128
FT = 64
FR_DEV = 16
F32 = jnp.float32
BF16 = jnp.bfloat16
EXP2_SCALE = math.log2(math.e) / math.sqrt(HD)
MASKED = -1e30
VMEM_LIMIT = 24 * 1024 * 1024
SWAP = [(0, 1), (1, 0)]
SHORT = pl.CostEstimate(flops=1024, bytes_accessed=1024, transcendentals=0)
ANY = pl.BlockSpec(memory_space=pl.ANY)
HBM = pl.BlockSpec(memory_space=pltpu.HBM)
VMEM = pl.BlockSpec(memory_space=pltpu.VMEM)


def params():
    return pltpu.CompilerParams(vmem_limit_bytes=VMEM_LIMIT)


def in_hbm(array):
    return pltpu.with_memory_space_constraint(array, pltpu.HBM)


def in_vmem(array):
    return pltpu.with_memory_space_constraint(array, pltpu.VMEM)


def quarter(other_seq, other_group):
    seq_part = lax.rem(lax.axis_index("seq"), 2)
    group = lax.axis_index("groups")
    return 2 * (1 - seq_part if other_seq else seq_part) + (1 - group if other_group else group)


def copy_all(pairs, sems):
    copies = [pltpu.make_async_copy(*pair, sems.at[index]) for index, pair in enumerate(pairs)]
    for copy in copies:
        copy.start()
    for copy in copies:
        copy.wait()


def exchange_order(seq_count):
    return [0, *range(seq_count // 2, seq_count), *range(1, seq_count // 2)]


def held_by(ids, stretch, owner, count):
    found = jnp.int32(0)
    for entry in range(count):
        frame = ids[stretch, entry]
        slot = frame - owner * FR_DEV
        found = jnp.where((slot >= 0) & (slot < FR_DEV), frame, found)
    return found


def pack_kernel(seq_count, low, parts, ids_in, keys, values, cur_keys, cur_values, weight, *rest):
    outs = rest[:seq_count]
    sibling, columns_out, ids, sems = rest[seq_count:]
    seq_index = lax.axis_index("seq")
    sub_index = lax.axis_index("sub")
    width = sibling.shape[1]
    block = columns_out.shape[1]
    count = cur_keys.shape[0]
    frame_count = 2 * seq_count
    copies = []

    def start(source, target):
        copy = pltpu.make_async_copy(source, target, sems.at[len(copies)])
        copy.start()
        copies.append(copy)
        return copy

    def columns_of(half):
        return pl.ds(pl.multiple_of(half * width, 128), width)

    listed = start(ids_in, ids)
    rows = count // parts
    for part, source in enumerate((cur_keys, cur_values)):
        for low_row in range(0, count, rows):
            target = sibling.at[pl.ds(part * count + low_row, rows), :]
            start(source.at[pl.ds(low_row, rows), columns_of(1 - sub_index)], target)
    first = pl.multiple_of(low + quarter(False, False) * block, 128)
    rows = weight.shape[0] // parts
    for part in range(parts):
        span = pl.ds(part * rows, rows)
        start(weight.at[span, pl.ds(first, block)], columns_out.at[span, :])
    listed.wait()
    for flip, out in zip(exchange_order(seq_count), outs):
        owner = seq_index * 2 + sub_index
        wanted = held_by(ids, lax.bitwise_xor(seq_index, flip), owner, frame_count) - owner * FR_DEV
        wanted = jnp.clip(wanted, 0, FR_DEV - 1)
        for turn in range(2):
            half = sub_index if turn == 0 else 1 - sub_index
            for part, source in enumerate((keys, values)):
                if flip == 0 and turn == 1:
                    target = sibling.at[pl.ds(2 * count + part * FT, FT), :]
                else:
                    target = out.at[pl.ds((2 * turn + part) * FT, FT), :]
                start(source.at[wanted, :, columns_of(half)], target)
    for copy in copies[1:]:
        copy.wait()


def pack(frame_ids, mem_keys, mem_values, cur_keys, cur_values, weight, low, share, seq_count):
    parts = 4
    width = mem_keys.shape[2] // 2
    rows = [2 * FT] + [4 * FT] * (seq_count - 1) + [2 * cur_keys.shape[0] + 2 * FT]
    shapes = [(count, width) for count in rows] + [(weight.shape[0], share)]
    return pl.pallas_call(
        functools.partial(pack_kernel, seq_count, low, parts),
        out_shape=[pltpu.VMEM(shape, BF16) for shape in shapes],
        in_specs=[HBM] * 6,
        out_specs=[VMEM] * len(shapes),
        scratch_shapes=[
            pltpu.SMEM(frame_ids.shape, jnp.int32),
            pltpu.SemaphoreType.DMA((1 + 4 * seq_count + 3 * parts,)),
        ],
        compiler_params=params(),
        name="pack",
        cost_estimate=pl.CostEstimate(flops=0, bytes_accessed=12 * 2**20, transcendentals=0),
    )(*map(in_hbm, (frame_ids, mem_keys, mem_values, cur_keys, cur_values, weight)))


def pass_on_kernel(*refs):
    arrays, out = refs[:-2], refs[-1]
    rows = out.shape[0] // len(arrays)
    for index, array in enumerate(arrays):
        out[pl.ds(index * rows, rows), :] = array[pl.ds(rows, rows), :]


def pass_on(arrays, after):
    rows, width = arrays[0].shape
    return pl.pallas_call(
        pass_on_kernel,
        out_shape=pltpu.VMEM((len(arrays) * rows // 2, width), BF16),
        in_specs=[VMEM] * len(arrays) + [ANY],
        out_specs=VMEM,
        compiler_params=params(),
        name="pass_on",
        cost_estimate=SHORT,
    )(*map(in_vmem, arrays), in_vmem(after))


def load_kernel(parts, seq_count, ids, counts, weight, after, out, mask, sems):
    rows = weight.shape[0] // parts
    spans = [pl.ds(part * rows, rows) for part in range(parts)]
    copies = [pltpu.make_async_copy(weight.at[span, :], out.at[span, :], sems.at[index]) for index, span in enumerate(spans)]
    for copy in copies:
        copy.start()
    seq_index = lax.axis_index("seq")
    sub_index = lax.axis_index("sub")
    slot = lax.broadcasted_iota(jnp.int32, (1, FT), 1)
    for index in range(2 * seq_count):
        turn, place = divmod(index, seq_count)
        source = lax.bitwise_xor(seq_index, exchange_order(seq_count)[place]) * 2
        owner = source + (sub_index if turn == 0 else 1 - sub_index)
        live = slot < counts[held_by(ids, seq_index, owner, 2 * seq_count)]
        mask[pl.ds(index, 1), :] = jnp.where(live, 0.0, MASKED).astype(F32)
    for copy in copies:
        copy.wait()


def load(frame_ids, frame_counts, weight, seq_count, after):
    parts = 8
    return pl.pallas_call(
        functools.partial(load_kernel, parts, seq_count),
        out_shape=[pltpu.VMEM(weight.shape, BF16), pltpu.VMEM((2 * seq_count, FT), F32)],
        in_specs=[pl.BlockSpec(memory_space=pltpu.SMEM)] * 2 + [HBM, ANY],
        out_specs=[VMEM, VMEM],
        scratch_shapes=[pltpu.SemaphoreType.DMA((parts,))],
        compiler_params=params(),
        name="load",
        cost_estimate=pl.CostEstimate(flops=0, bytes_accessed=2 * weight.size, transcendentals=0),
    )(*map(in_hbm, (frame_ids, frame_counts, weight)), in_vmem(after))


def gate(array, after):
    return pl.pallas_call(
        lambda *refs: None,
        in_specs=[ANY, ANY],
        out_specs=ANY,
        out_shape=jax.ShapeDtypeStruct(array.shape, array.dtype),
        input_output_aliases={0: 0},
        compiler_params=params(),
        name="gate",
        cost_estimate=SHORT,
    )(in_vmem(array), in_vmem(after))


def copied_kernel(array, after, out):
    out[...] = array[...]


def copied(array, after):
    return pl.pallas_call(
        copied_kernel,
        in_specs=[VMEM, ANY],
        out_specs=VMEM,
        out_shape=pltpu.VMEM(array.shape, array.dtype),
        compiler_params=params(),
        name="copied",
        cost_estimate=SHORT,
    )(in_vmem(array), in_vmem(after))


def dot_t(left, right):
    return lax.dot_general(left, right, (((1,), (1,)), ((), ())), preferred_element_type=F32)


def wide(column, count):
    return jnp.concatenate([column] * count, axis=1)


def with_ones(values):
    return jnp.concatenate([values, jnp.ones_like(values)], axis=1)


def current_kernel(step, queries, own_keys, own_values, sibling, out, lse, q, own_k, own_v, sems):
    heads, rows, _ = out.shape
    count = own_k.shape[0]
    half = pl.ds(pl.multiple_of(lax.axis_index("sub") * q.shape[1], 128), q.shape[1])
    copy_all(
        [(queries.at[:, half], q), (own_keys.at[:, half], own_k), (own_values.at[:, half], own_v)],
        sems,
    )

    @pl.loop(0, heads)
    def _(head):
        columns = pl.ds(pl.multiple_of(head * HD, HD), HD)
        keys = jnp.concatenate([own_k[:, columns], sibling[pl.ds(0, count), columns]], axis=0)
        values = with_ones(jnp.concatenate([own_v[:, columns], sibling[pl.ds(count, count), columns]], axis=0))
        for low in range(0, rows, step):
            span = pl.ds(low, step)
            scores = dot_t(q[span, columns], keys)
            row_max = jnp.broadcast_to(jnp.max(scores, axis=1, keepdims=True), (step, HD))
            weights = jnp.exp2((scores - wide(row_max, 2 * count // HD)) * EXP2_SCALE).astype(BF16)
            product = jnp.dot(weights, values, preferred_element_type=F32)
            total = product[:, HD:]
            out[head, span, :] = product[:, :HD] / total
            lse[head, span, :] = row_max * EXP2_SCALE + jnp.log2(total)


def attend_current(queries, cur_keys, cur_values, sibling, heads):
    rows = queries.shape[0]
    keys = cur_keys.shape[0]
    return pl.pallas_call(
        functools.partial(current_kernel, 512),
        in_specs=[HBM] * 3 + [VMEM],
        out_specs=[VMEM] * 3,
        out_shape=[pltpu.VMEM((heads, rows, HD), F32)] * 2 + [pltpu.VMEM((rows, heads * HD), BF16)],
        scratch_shapes=[pltpu.VMEM((keys, heads * HD), BF16)] * 2 + [pltpu.SemaphoreType.DMA((3,))],
        compiler_params=params(),
        name="attend_current",
        cost_estimate=pl.CostEstimate(
            flops=60 * heads * rows * 2 * keys * HD, bytes_accessed=heads * rows * HD * 12, transcendentals=heads * rows * 2 * keys
        ),
    )(in_hbm(queries), in_hbm(cur_keys), in_hbm(cur_values), in_vmem(sibling))


def frames_kernel(heads, half_of, state_half_of, first, starts, final, bias, q, held, lse, *rest):
    frames = rest[: len(starts)]
    outs = rest[-1:] if final else rest[-2:]
    count, rows = len(starts), outs[0].shape[-2]

    def rows_of(half):
        return pl.ds(pl.multiple_of(half() * rows, rows), rows)

    span, state_span = rows_of(half_of), rows_of(state_half_of)
    mask = jnp.concatenate([bias[pl.ds(first + index, 1), :] for index in range(count)], axis=1)

    def gathered(head, part):
        columns = pl.ds(head * HD, HD)
        return jnp.concatenate(
            [frame[pl.ds(start + part * FT, FT), columns] for frame, start in zip(frames, starts)], axis=0
        )

    def scores_of(head):
        return dot_t(q[span, pl.ds(head * HD, HD)], gathered(head, 0))

    def finish(head, scores):
        scores = scores * EXP2_SCALE + mask
        old = lse[head, state_span, :]
        new_max = jnp.maximum(old, jnp.max(scores, axis=1, keepdims=True))
        weights = jnp.exp2(scores - wide(new_max, count * FT // HD)).astype(BF16)
        product = jnp.dot(weights, with_ones(gathered(head, 1)), preferred_element_type=F32)
        scale = jnp.exp2(old - new_max)
        total = scale + product[:, HD:]
        top = (held[head, state_span, :] * scale + product[:, :HD]) / total
        if final:
            outs[0][:, pl.ds(head * HD, HD)] = top.astype(BF16)
        else:
            outs[0][head] = top
            outs[1][head] = new_max + jnp.log2(total)

    scores = scores_of(0)
    for head in range(heads):
        following = scores_of(head + 1) if head + 1 < heads else None
        finish(head, scores)
        scores = following


def far_half():
    return 1 - lax.axis_index("head")


def near_half():
    return lax.axis_index("head")


def attend_frames(name, half, bias, first, q, held, lse, frames, starts, final, after=()):
    heads, state_rows, _ = held.shape
    rows = q.shape[0] // 2
    state_half = half if state_rows > rows else lambda: jnp.int32(0)
    operands = [bias, q, held, lse, *frames]
    if final:
        out_shape = [pltpu.VMEM((rows, heads * HD), BF16)]
    else:
        out_shape = [pltpu.VMEM((heads, rows, HD), F32)] * 2
    outs = pl.pallas_call(
        functools.partial(frames_kernel, heads, half, state_half, first, tuple(starts), final),
        in_specs=[VMEM] * len(operands) + [ANY] * len(after),
        out_specs=[VMEM] * len(out_shape),
        out_shape=out_shape,
        compiler_params=params(),
        name=name,
        cost_estimate=SHORT,
    )(*map(in_vmem, operands), *map(in_vmem, after))
    return outs[0] if final else outs


def both(mine, other):
    first, second = mine[...], other[...]
    return jnp.where(
        lax.axis_index("sub") == 0,
        jnp.concatenate([first, second], axis=1),
        jnp.concatenate([second, first], axis=1),
    )


def project_kernel(step, mine, other, weight, *rest):
    out = rest[-1]
    rows = both(mine, other)

    @pl.loop(0, out.shape[1] // step)
    def _(index):
        columns = pl.ds(pl.multiple_of(index * step, step), step)
        out[:, columns] = jnp.dot(rows, weight[:, columns], preferred_element_type=F32).astype(BF16)


def unshared_columns(low, share):
    return pl.ds(0, low), pl.ds(pl.multiple_of(low + quarter(True, True) * share, 128), share)


def unshared_kernel(low, mine, other, weight, *rest):
    out = rest[-1]
    rows = both(mine, other)
    start = 0
    for columns in unshared_columns(low, out.shape[1] - low):
        out[:, pl.ds(start, columns.size)] = jnp.dot(rows, weight[:, columns], preferred_element_type=F32).astype(BF16)
        start += columns.size


def project_call(kernel, name, mine, other, weight, width, after):
    return pl.pallas_call(
        kernel,
        in_specs=[VMEM] * 3 + [ANY] * len(after),
        out_specs=VMEM,
        out_shape=pltpu.VMEM((mine.shape[0], width), BF16),
        compiler_params=params(),
        name=name,
        cost_estimate=SHORT,
    )(*map(in_vmem, (mine, other, weight, *after)))


def project(mine, other, weight, after):
    return project_call(functools.partial(project_kernel, 512), "project", mine, other, weight, weight.shape[1], after)


def project_unshared(mine, other, weight, low, share, after):
    kernel = functools.partial(unshared_kernel, low)
    return project_call(kernel, "project_unshared", mine, other, weight, low + share, after)


def write_blocks(blocks, out, scratch, sems):
    copies, start = [], 0
    for index, (block, low) in enumerate(blocks):
        span = pl.ds(start, block.shape[1])
        scratch[:, span] = block.astype(BF16)
        copy = pltpu.make_async_copy(scratch.at[:, span], out.at[:, pl.ds(low, block.shape[1])], sems.at[index])
        copy.start()
        copies.append(copy)
        start += block.shape[1]
    for copy in copies:
        copy.wait()


def remote_kernel(first, other_seq, other_group, terms, mine, other, weight, total, out, scratch, sems):
    block = weight.shape[1]
    low = pl.multiple_of(first + quarter(other_seq, other_group) * block, 128)
    product = jnp.dot(both(mine, other), weight[...], preferred_element_type=F32)
    write_blocks([(terms[:, pl.ds(low, block)].astype(F32) + product, low)], out, scratch, sems)


def add_kernel(low, terms, came, total, out, scratch, sems):
    blocks, start = [], 0
    for columns in unshared_columns(low, came.shape[1] - low):
        block = terms[:, columns].astype(F32) + came[:, pl.ds(start, columns.size)].astype(F32)
        blocks.append((block, columns.start))
        start += columns.size
    write_blocks(blocks, out, scratch, sems)


def finish_block(kernel, name, operands, total, rows, width, block):
    count = len(operands)
    if total is None:
        body = lambda *refs: kernel(*refs[:count], None, *refs[count:])
        totals, aliases = [], {}
    else:
        body, totals, aliases = kernel, [in_hbm(total)], {count: 0}
    return pl.pallas_call(
        body,
        in_specs=[VMEM] * count + [HBM] * len(totals),
        out_specs=HBM,
        out_shape=pltpu.HBM((rows, width), BF16),
        input_output_aliases=aliases,
        scratch_shapes=[pltpu.VMEM((rows, block), BF16), pltpu.SemaphoreType.DMA((2,))],
        compiler_params=params(),
        name=name,
        cost_estimate=SHORT,
    )(*map(in_vmem, operands), *totals)


def add_remote(terms, mine, other, weight, first, other_seq, other_group, total):
    kernel = functools.partial(remote_kernel, first, other_seq, other_group)
    return finish_block(kernel, "add_remote", (terms, mine, other, weight), total, *terms.shape, weight.shape[1])


def add_unshared(terms, came, low, total):
    kernel = functools.partial(add_kernel, low)
    return finish_block(kernel, "add_unshared", (terms, came), total, *terms.shape, came.shape[1])


def local(queries, cur_keys, cur_values, mem_keys, mem_values, frame_ids, frame_counts, out_weight):
    seq_count = lax.axis_size("seq")
    heads = queries.shape[1] // HD // 2
    keys = cur_keys.shape[0]
    out_cols = out_weight.shape[1]
    share = out_cols // 5 // 128 * 128
    low = out_cols - 4 * share

    *sends, to_sibling, columns = pack(
        frame_ids, mem_keys, mem_values, cur_keys, cur_values, out_weight, low, share, seq_count
    )
    mine = [sends[0]]
    for flip, sent in list(zip(exchange_order(seq_count), sends))[1:]:
        mine.append(lax.ppermute(sent, "seq", [(index, index ^ flip) for index in range(seq_count)]))
    columns = lax.ppermute(columns, "head", SWAP)
    sibling = lax.ppermute(to_sibling, "sub", SWAP)

    held, lse, q = attend_current(queries, cur_keys, cur_values, sibling, heads)
    weight, bias = load(frame_ids, frame_counts, out_weight, seq_count, lse)
    passed = pass_on(mine[1:], weight)
    theirs = lax.ppermute(passed, "sub", SWAP)
    others = [sibling] + [theirs] * (seq_count - 1)
    starts = [2 * keys] + [2 * FT * index for index in range(seq_count - 1)]

    state = attend_frames("far_first", far_half, bias, 0, q, held, lse, mine, [0] * seq_count, False, (passed,))
    far = attend_frames("far_last", far_half, bias, seq_count, q, *state, others, starts, True)
    came_mine = lax.ppermute(far, "head", SWAP)
    far_sibling = lax.ppermute(far, "sub", SWAP)
    group_columns = lax.ppermute(columns, "groups", SWAP)
    columns_copy = copied(columns, far)
    seq_columns = lax.ppermute(columns_copy, "seq", [(index, index ^ 1) for index in range(seq_count)])
    starts = [0] * seq_count + starts
    near = attend_frames("near", near_half, bias, 0, q, held, lse, mine + others, starts, True, (columns_copy,))
    near_sibling = lax.ppermute(near, "sub", SWAP)

    term = project_unshared(far, far_sibling, weight, low, share, (near,))
    came = lax.ppermute(term, "head", SWAP)
    came_mine = gate(came_mine, term)
    came_other = lax.ppermute(came_mine, "sub", SWAP)
    terms = project(near, near_sibling, weight, (came_mine,))

    arrived = (terms, came_mine, came_other)
    total = add_remote(*arrived, columns, low, False, False, None)
    total = add_remote(*arrived, group_columns, low, False, True, total)
    total = add_remote(*arrived, seq_columns, low, True, False, total)
    return add_unshared(terms, came, low, total)


def local_any(queries, cur_keys, cur_values, mem_keys, mem_values, frame_ids, frame_counts, out_weight):
    seq_count = lax.axis_size("seq")
    sub_count = lax.axis_size("sub")
    seq_index = lax.axis_index("seq")
    owner_self = seq_index * sub_count + lax.axis_index("sub")
    row_count, col_count = queries.shape
    heads = col_count // HD
    mine = row_count // sub_count
    wanted = jnp.sum(jnp.where(frame_ids // FR_DEV == owner_self, frame_ids, 0), axis=1) - owner_self * FR_DEV
    own_list = lax.dynamic_index_in_dim(frame_ids, seq_index, 0, keepdims=False)
    owners = jnp.arange(seq_count * sub_count, dtype=jnp.int32)
    hit = (own_list // FR_DEV)[None, :] == owners[:, None]
    got_ids = jnp.sum(jnp.where(hit, own_list[None, :], 0), axis=1).reshape(seq_count, sub_count).T.reshape(-1)
    live = jnp.arange(FT, dtype=jnp.int32)[None, :] < jnp.take(frame_counts, got_ids)[:, None]

    def spread(cached, current):
        sent = lax.all_to_all(jnp.take(cached, wanted, axis=0), "seq", split_axis=0, concat_axis=0, tiled=True)
        far = lax.all_gather(sent, "sub").reshape(-1, heads, HD)
        return jnp.concatenate([lax.all_gather(current, "sub").reshape(-1, heads, HD), far], axis=0)

    keys, values = spread(mem_keys, cur_keys), spread(mem_values, cur_values)
    key_live = jnp.concatenate([jnp.ones((keys.shape[0] - live.size,), bool), live.reshape(-1)])
    start = lax.axis_index("sub") * mine
    query_heads = lax.dynamic_slice_in_dim(queries, start, mine, 0).reshape(mine, heads, HD)
    scores = jnp.einsum("qhd,khd->hqk", query_heads, keys, preferred_element_type=F32) / math.sqrt(HD)
    scores = jnp.where(key_live[None, None, :], scores, -jnp.inf)
    expo = jnp.exp(scores - jnp.max(scores, axis=-1, keepdims=True))
    total = jnp.sum(expo, axis=-1)
    weighted = jnp.einsum("hqk,khd->qhd", expo.astype(BF16), values, preferred_element_type=F32)
    attended = (weighted / total.T[:, :, None]).reshape(mine, col_count).astype(BF16)
    attended = lax.all_gather(attended, "sub", axis=0, tiled=True)
    term = jnp.dot(attended, out_weight, preferred_element_type=F32).astype(BF16)
    return lax.psum_scatter(term, "head", scatter_dimension=0, tiled=True)


def solution(mesh):
    in_specs = (
        P(("groups", "seq"), "head"),
        P(("groups", "seq", "sub"), "head"),
        P(("groups", "seq", "sub"), "head"),
        P(("groups", "seq", "sub"), None, "head"),
        P(("groups", "seq", "sub"), None, "head"),
        P("groups", None),
        P("groups"),
        P("head", "sub"),
    )
    out_specs = P(("groups", "seq", "head"), "sub")

    def apply(queries, *rest):
        heads = queries.shape[1] // mesh.shape["head"] // HD
        paired = heads % 2 == 0 and mesh.shape["seq"] in (2, 4, 8)
        paired = paired and all(mesh.shape[axis] == 2 for axis in ("groups", "head", "sub"))
        body = local if paired else local_any
        return jax.shard_map(body, mesh=mesh, in_specs=in_specs, out_specs=out_specs, check_vma=False)(queries, *rest)

    return apply
```

profile of v0, /device:TPU:20, one launch (start us, length us, event | category | flops | bytes accessed | tf_op | source)
XLA Modules:
  0.0 79.0 jit_solution(15823721457189876972)
XLA Ops:
  0.0 2.6 %pack.1 = (bf16[128,640]{1,0:T(8,128)(2,1)S(1)}, bf16[256,640]{1,0:T(8,128)(2,1)S(1)}, bf16[256,640]{1,0:T(8,128)(2,1)S(1)}, bf16[256,640]{1,0:T(8,128)(2,1)S(1)...) custom-call(s32[4,8]{1,0:T(4,128)} %ids.1, bf16[16,64,1280]{2,1,0:T(8,128)(2,1)} %keys.1, ...), custom_call_target="tpu_custom_call" | custom-call | bytes 12582912 | tf_op jit(solution)/shard_map/pack/pallas_call | solution.py:118
  2.7 0.4 collective-permute-start.1
  3.1 2.7 %collective-permute-start.2 = (bf16[256,640]{1,0:T(8,128)(2,1)S(1)}, bf16[256,640]{1,0:T(8,128)(2,1)S(1)}, u32[]{:S(2)}, u32[]{:S(2)}) collective-permute-start(bf16[256,640]{1,0:T(8,128)(2,1)S(1)} %get-tuple-element.25), channel_id=1, source_target_pairs={{0,12},{4,8},{8,4},{12,0},{1,13},{5,9},{9,5},{13,1},{2,14},{6,10},... | collective-permute-start | bytes 983048 | tf_op jit(solution)/shard_map/ppermute | solution.py:465
  5.8 1.3 %collective-permute-start.3 = (bf16[256,640]{1,0:T(8,128)(2,1)S(1)}, bf16[256,640]{1,0:T(8,128)(2,1)S(1)}, u32[]{:S(2)}, u32[]{:S(2)}) collective-permute-start(bf16[256,640]{1,0:T(8,128)(2,1)S(1)} %get-tuple-element.26), channel_id=1, source_target_pairs={{0,4},{4,0},{8,12},{12,8},{1,5},{5,1},{9,13},{13,9},{2,6},{6,2},{1... | collective-permute-start | bytes 983048 | tf_op jit(solution)/shard_map/ppermute | solution.py:465
  7.2 1.5 %collective-permute-start.5 = (bf16[1280,512]{1,0:T(8,128)(2,1)S(1)}, bf16[1280,512]{1,0:T(8,128)(2,1)S(1)}, u32[]{:S(2)}, u32[]{:S(2)}) collective-permute-start(bf16[1280,512]{1,0:T(8,128)(2,1)S(1)} %get-tuple-element.28), channel_id=1, source_target_pairs={{0,2},{2,0},{1,3},{3,1},{4,6},{6,4},{5,7},{7,5},{8,10},{10,8},{9,1... | collective-permute-start | bytes 3932168 | tf_op jit(solution)/shard_map/ppermute | solution.py:466
  8.6 11.3 %attend_current.1 = (f32[5,1024,128]{2,1,0:T(8,128)S(1)}, f32[5,1024,128]{2,1,0:T(8,128)S(1)}, bf16[1024,640]{1,0:T(8,128)(2,1)S(1)}) custom-call(bf16[1024,1280]{1,0:T(8,128)(2,1)} %queries.1, bf16[512,1280]{1,0:T(8,128)(2,1)} %own_keys.1, bf16[512,1280]{1,0:T(8,128)(2,1)} %own_values.1, bf16[1152,640]{1,0:T(8,128)(2,1)S(1)} %collective-permute-done.sibling.rest_0_.rest_4_), custom_call_target="tpu_custom_call" | custom-call | flops 40265318400 | bytes 7864320 | tf_op jit(solution)/shard_map/attend_current/pallas_call | solution.py:255
  19.9 3.6 %load.1 = (bf16[1280,2560]{1,0:T(8,128)(2,1)S(1)}, f32[8,64]{1,0:T(8,128)S(1)}) custom-call(s32[4,8]{1,0:T(4,128)} %ids.1, s32[128]{0:T(128)} %counts.1, bf16[1280,2560]{1,0:T(8,128)(2,1)} %weight.3, f32[5,1024,128]{2,1,0:T(8,128)S(1)} %get-tuple-element.19.after.lse), custom_call_target="tpu_custom_call" | custom-call | bytes 6553600 | tf_op jit(solution)/shard_map/load/pallas_call | solution.py:174
  23.6 1.6 %collective-permute-done.1.refs_0_.rest_1_ = bf16[256,640]{1,0:T(8,128)(2,1)S(1)} collective-permute-done((bf16[256,640]{1,0:T(8,128)(2,1)S(1)}, bf16[256,640]{1,0:T(8,128)(2,1)S(1)}, u32[]{:S(2)}, u32[]{:S(2)}) %collective-permute-start.1) | collective-permute-done | bytes 327712 | tf_op jit(solution)/shard_map/ppermute | solution.py:465
  25.2 9.6 %collective-permute-done.2.refs_1_.rest_2_ = bf16[256,640]{1,0:T(8,128)(2,1)S(1)} collective-permute-done((bf16[256,640]{1,0:T(8,128)(2,1)S(1)}, bf16[256,640]{1,0:T(8,128)(2,1)S(1)}, u32[]{:S(2)}, u32[]{:S(2)}) %collective-permute-start.2) | collective-permute-done | bytes 327712 | tf_op jit(solution)/shard_map/ppermute | solution.py:465
  35.0 1.4 %far_first.1 = (f32[5,512,128]{2,1,0:T(8,128)S(1)}, f32[5,512,128]{2,1,0:T(8,128)S(1)}) custom-call(f32[8,64]{1,0:T(8,128)S(1)} %get-tuple-element.20.bias, bf16[1024,640]{1,0:T(8,128)(2,1)S(1)} %get-tuple-element.21.q, f32[5,1024,128]{2,1,0:T(8,128)S(1)} %get-tuple-element.22.held, f32[5,1024,128]{2,1,0:T(8,128)S(1)} %get-tuple-element.19.after.lse, ...), custom_call_target="tpu_custom_call" | custom-call | flops 1024 | bytes 1024 | tf_op jit(solution)/shard_map/far_first/pallas_call | solution.py:328
  36.8 1.4 %far_last.1.after.mine = bf16[512,640]{1,0:T(8,128)(2,1)S(1)} custom-call(f32[8,64]{1,0:T(8,128)S(1)} %get-tuple-element.20.bias, bf16[1024,640]{1,0:T(8,128)(2,1)S(1)} %get-tuple-element.21.q, f32[5,512,128]{2,1,0:T(8,128)S(1)} %get-tuple-element.29.held, f32[5,512,128]{2,1,0:T(8,128)S(1)} %get-tuple-element.30.lse, ...), custom_call_target="tpu_custom_call" | custom-call | flops 1024 | bytes 1024 | tf_op jit(solution)/shard_map/far_last/pallas_call | solution.py:328
  38.4 1.5 %collective-permute-start.7 = (bf16[512,640]{1,0:T(8,128)(2,1)S(1)}, bf16[512,640]{1,0:T(8,128)(2,1)S(1)}, u32[]{:S(2)}, u32[]{:S(2)}) collective-permute-start(bf16[512,640]{1,0:T(8,128)(2,1)S(1)} %far_last.1.after.mine), channel_id=1, source_target_pairs={{0,2},{2,0},{1,3},{3,1},{4,6},{6,4},{5,7},{7,5},{8,10},{10,8},{9,1... | collective-permute-start | bytes 1966088 | tf_op jit(solution)/shard_map/ppermute | solution.py:478
  40.0 0.5 collective-permute-start.12
  40.6 2.1 %near.1.rest_0_.mine = bf16[512,640]{1,0:T(8,128)(2,1)S(1)} custom-call(f32[8,64]{1,0:T(8,128)S(1)} %get-tuple-element.20.bias, bf16[1024,640]{1,0:T(8,128)(2,1)S(1)} %get-tuple-element.21.q, f32[5,1024,128]{2,1,0:T(8,128)S(1)} %get-tuple-element.22.held, f32[5,1024,128]{2,1,0:T(8,128)S(1)} %get-tuple-element.19.after.lse, ...), custom_call_target="tpu_custom_call" | custom-call | flops 1024 | bytes 1024 | tf_op jit(solution)/shard_map/near/pallas_call | solution.py:328
  42.7 1.6 %project_unshared.1.refs_1_ = bf16[512,1024]{1,0:T(8,128)(2,1)S(1)} custom-call(bf16[512,640]{1,0:T(8,128)(2,1)S(1)} %far_last.1.after.mine, bf16[512,640]{1,0:T(8,128)(2,1)S(1)} %collective-permute-done.8.other, bf16[1280,2560]{1,0:T(8,128)(2,1)S(1)} %get-tuple-element.27.refs_3_.weight, bf16[512,640]{1,0:T(8,128)(2,1)S(1)} %near.1.rest_0_.mine), custom_call_target="tpu_custom_call" | custom-call | flops 1024 | bytes 1024 | tf_op jit(solution)/shard_map/project_unshared/pallas_call | solution.py:373
  44.3 0.6 collective-permute-start.9
  44.9 11.1 %collective-permute-done.7.refs_0_ = bf16[512,640]{1,0:T(8,128)(2,1)S(1)} collective-permute-done((bf16[512,640]{1,0:T(8,128)(2,1)S(1)}, bf16[512,640]{1,0:T(8,128)(2,1)S(1)}, u32[]{:S(2)}, u32[]{:S(2)}) %collective-permute-start.7) | collective-permute-done | bytes 655392 | tf_op jit(solution)/shard_map/ppermute | solution.py:478
  56.0 4.4 %project.1.refs_0_.terms = bf16[512,2560]{1,0:T(8,128)(2,1)S(1)} custom-call(bf16[512,640]{1,0:T(8,128)(2,1)S(1)} %near.1.rest_0_.mine, bf16[512,640]{1,0:T(8,128)(2,1)S(1)} %collective-permute-done.6.other, bf16[1280,2560]{1,0:T(8,128)(2,1)S(1)} %get-tuple-element.27.refs_3_.weight, bf16[512,640]{1,0:T(8,128)(2,1)S(1)} %gate.1.rest_0_.refs_1_.mine), custom_call_target="tpu_custom_call" | custom-call | flops 1024 | bytes 1024 | tf_op jit(solution)/shard_map/project/pallas_call | solution.py:373
  60.4 1.7 %add_remote.3.total = bf16[512,2560]{1,0:T(8,128)(2,1)} custom-call(bf16[512,2560]{1,0:T(8,128)(2,1)S(1)} %project.1.refs_0_.terms, bf16[512,640]{1,0:T(8,128)(2,1)S(1)} %gate.1.rest_0_.refs_1_.mine, bf16[512,640]{1,0:T(8,128)(2,1)S(1)} %collective-permute-done.10.refs_2_.other, bf16[1280,512]{1,0:T(8,128)(2,1)S(1)} %collective-permute-done.5.array.refs_3_), custom_call_target="tpu_custom_call" | custom-call | flops 1024 | bytes 1024 | tf_op jit(solution)/shard_map/add_remote/pallas_call | solution.py:429
  62.1 8.6 %collective-permute-done.12.weight = bf16[1280,512]{1,0:T(8,128)(2,1)S(1)} collective-permute-done((bf16[1280,512]{1,0:T(8,128)(2,1)S(1)}, bf16[1280,512]{1,0:T(8,128)(2,1)S(1)}, u32[]{:S(2)}, u32[]{:S(2)}) %collective-permute-start.12) | collective-permute-done | bytes 1310752 | tf_op jit(solution)/shard_map/ppermute | solution.py:480
  70.7 1.7 %add_remote.4.total = bf16[512,2560]{1,0:T(8,128)(2,1)} custom-call(bf16[512,2560]{1,0:T(8,128)(2,1)S(1)} %project.1.refs_0_.terms, bf16[512,640]{1,0:T(8,128)(2,1)S(1)} %gate.1.rest_0_.refs_1_.mine, bf16[512,640]{1,0:T(8,128)(2,1)S(1)} %collective-permute-done.10.refs_2_.other, ...), custom_call_target="tpu_custom_call", output_to_operand_aliasing={{}: (4, {})} | custom-call | flops 1024 | bytes 1024 | tf_op jit(solution)/shard_map/add_remote/pallas_call | solution.py:429
  72.4 1.7 %add_remote.5.total = bf16[512,2560]{1,0:T(8,128)(2,1)} custom-call(bf16[512,2560]{1,0:T(8,128)(2,1)S(1)} %project.1.refs_0_.terms, bf16[512,640]{1,0:T(8,128)(2,1)S(1)} %gate.1.rest_0_.refs_1_.mine, bf16[512,640]{1,0:T(8,128)(2,1)S(1)} %collective-permute-done.10.refs_2_.other, ...), custom_call_target="tpu_custom_call", output_to_operand_aliasing={{}: (4, {})} | custom-call | flops 1024 | bytes 1024 | tf_op jit(solution)/shard_map/add_remote/pallas_call | solution.py:429
  74.1 3.8 %collective-permute-done.9.came = bf16[512,1024]{1,0:T(8,128)(2,1)S(1)} collective-permute-done((bf16[512,1024]{1,0:T(8,128)(2,1)S(1)}, bf16[512,1024]{1,0:T(8,128)(2,1)S(1)}, u32[]{:S(2)}, u32[]{:S(2)}) %collective-permute-start.9) | collective-permute-done | bytes 1048608 | tf_op jit(solution)/shard_map/ppermute | solution.py:488
  77.9 1.1 %add_unshared.1 = bf16[512,2560]{1,0:T(8,128)(2,1)} custom-call(bf16[512,2560]{1,0:T(8,128)(2,1)S(1)} %project.1.refs_0_.terms, bf16[512,1024]{1,0:T(8,128)(2,1)S(1)} %collective-permute-done.9.came, bf16[512,2560]{1,0:T(8,128)(2,1)} %add_remote.5.total), custom_call_target="tpu_custom_call", output_to_operand_aliasing={{}: (2, {})} | custom-call | flops 1024 | bytes 1024 | tf_op jit(solution)/shard_map/add_unshared/pallas_call | solution.py:429
  (17 shorter events, 1.0 us)
Async XLA Ops:
  2.6 6.0 %collective-permute-start = (bf16[1152,640]{1,0:T(8,128)(2,1)S(1)}, bf16[1152,640]{1,0:T(8,128)(2,1)S(1)}, u32[]{:S(2)}, u32[]{:S(2)}) collective-permute-start(bf16[1152,640]{1,0:T(8,128)(2,1)S(1)} %get-tuple-element.18), channel_id=1, source_target_pairs={{0,1},{1,0},{2,3},{3,2},{4,5},{5,4},{6,7},{7,6},{8,9},{9,8},{10,11... | collective-permute-start | bytes 4423688 | tf_op jit(solution)/shard_map/ppermute | solution.py:467
  2.7 22.5 %collective-permute-start.1 = (bf16[256,640]{1,0:T(8,128)(2,1)S(1)}, bf16[256,640]{1,0:T(8,128)(2,1)S(1)}, u32[]{:S(2)}, u32[]{:S(2)}) collective-permute-start(bf16[256,640]{1,0:T(8,128)(2,1)S(1)} %get-tuple-element.24), channel_id=1, source_target_pairs={{0,8},{4,12},{8,0},{12,4},{1,9},{5,13},{9,1},{13,5},{2,10},{6,14},... | collective-permute-start | bytes 983048 | tf_op jit(solution)/shard_map/ppermute | solution.py:465
  3.1 31.7 %collective-permute-start.2 = (bf16[256,640]{1,0:T(8,128)(2,1)S(1)}, bf16[256,640]{1,0:T(8,128)(2,1)S(1)}, u32[]{:S(2)}, u32[]{:S(2)}) collective-permute-start(bf16[256,640]{1,0:T(8,128)(2,1)S(1)} %get-tuple-element.25), channel_id=1, source_target_pairs={{0,12},{4,8},{8,4},{12,0},{1,13},{5,9},{9,5},{13,1},{2,14},{6,10},... | collective-permute-start | bytes 983048 | tf_op jit(solution)/shard_map/ppermute | solution.py:465
  5.8 29.0 %collective-permute-start.3 = (bf16[256,640]{1,0:T(8,128)(2,1)S(1)}, bf16[256,640]{1,0:T(8,128)(2,1)S(1)}, u32[]{:S(2)}, u32[]{:S(2)}) collective-permute-start(bf16[256,640]{1,0:T(8,128)(2,1)S(1)} %get-tuple-element.26), channel_id=1, source_target_pairs={{0,4},{4,0},{8,12},{12,8},{1,5},{5,1},{9,13},{13,9},{2,6},{6,2},{1... | collective-permute-start | bytes 983048 | tf_op jit(solution)/shard_map/ppermute | solution.py:465
  7.2 32.8 %collective-permute-start.5 = (bf16[1280,512]{1,0:T(8,128)(2,1)S(1)}, bf16[1280,512]{1,0:T(8,128)(2,1)S(1)}, u32[]{:S(2)}, u32[]{:S(2)}) collective-permute-start(bf16[1280,512]{1,0:T(8,128)(2,1)S(1)} %get-tuple-element.28), channel_id=1, source_target_pairs={{0,2},{2,0},{1,3},{3,1},{4,6},{6,4},{5,7},{7,5},{8,10},{10,8},{9,1... | collective-permute-start | bytes 3932168 | tf_op jit(solution)/shard_map/ppermute | solution.py:466
  34.9 1.9 %collective-permute-start.4 = (bf16[384,640]{1,0:T(8,128)(2,1)S(1)}, bf16[384,640]{1,0:T(8,128)(2,1)S(1)}, u32[]{:S(2)}, u32[]{:S(2)}) collective-permute-start(bf16[384,640]{1,0:T(8,128)(2,1)S(1)} %pass_on.1.rest_4_), channel_id=1, source_target_pairs={{0,1},{1,0},{2,3},{3,2},{4,5},{5,4},{6,7},{7,6},{8,9},{9,8},{10,11... | collective-permute-start | bytes 1474568 | tf_op jit(solution)/shard_map/ppermute | solution.py:472
  38.2 4.5 %collective-permute-start.8 = (bf16[512,640]{1,0:T(8,128)(2,1)S(1)}, bf16[512,640]{1,0:T(8,128)(2,1)S(1)}, u32[]{:S(2)}, u32[]{:S(2)}) collective-permute-start(bf16[512,640]{1,0:T(8,128)(2,1)S(1)} %far_last.1.after.mine), channel_id=1, source_target_pairs={{0,1},{1,0},{2,3},{3,2},{4,5},{5,4},{6,7},{7,6},{8,9},{9,8},{10,11... | collective-permute-start | bytes 1966088 | tf_op jit(solution)/shard_map/ppermute | solution.py:479
  38.4 17.6 %collective-permute-start.7 = (bf16[512,640]{1,0:T(8,128)(2,1)S(1)}, bf16[512,640]{1,0:T(8,128)(2,1)S(1)}, u32[]{:S(2)}, u32[]{:S(2)}) collective-permute-start(bf16[512,640]{1,0:T(8,128)(2,1)S(1)} %far_last.1.after.mine), channel_id=1, source_target_pairs={{0,2},{2,0},{1,3},{3,1},{4,6},{6,4},{5,7},{7,5},{8,10},{10,8},{9,1... | collective-permute-start | bytes 1966088 | tf_op jit(solution)/shard_map/ppermute | solution.py:478
  40.0 30.8 %collective-permute-start.12 = (bf16[1280,512]{1,0:T(8,128)(2,1)S(1)}, bf16[1280,512]{1,0:T(8,128)(2,1)S(1)}, u32[]{:S(2)}, u32[]{:S(2)}) collective-permute-start(bf16[1280,512]{1,0:T(8,128)(2,1)S(1)} %collective-permute-done.5.array.refs_3_), channel_id=1, source_target_pairs={{0,16},{16,0},{1,17},{17,1},{2,18},{18,2},{3,19},{19,3},{4,20},{20... | collective-permute-start | bytes 3932168 | tf_op jit(solution)/shard_map/ppermute | solution.py:480
  40.5 31.9 %collective-permute-start.11 = (bf16[1280,512]{1,0:T(8,128)(2,1)S(1)}, bf16[1280,512]{1,0:T(8,128)(2,1)S(1)}, u32[]{:S(2)}, u32[]{:S(2)}) collective-permute-start(bf16[1280,512]{1,0:T(8,128)(2,1)S(1)} %copied.1.rest_8_), channel_id=1, source_target_pairs={{0,4},{4,0},{8,12},{12,8},{1,5},{5,1},{9,13},{13,9},{2,6},{6,2},{1... | collective-permute-start | bytes 3932168 | tf_op jit(solution)/shard_map/ppermute | solution.py:482
  44.3 33.6 %collective-permute-start.9 = (bf16[512,1024]{1,0:T(8,128)(2,1)S(1)}, bf16[512,1024]{1,0:T(8,128)(2,1)S(1)}, u32[]{:S(2)}, u32[]{:S(2)}) collective-permute-start(bf16[512,1024]{1,0:T(8,128)(2,1)S(1)} %project_unshared.1.refs_1_), channel_id=1, source_target_pairs={{0,2},{2,0},{1,3},{3,1},{4,6},{6,4},{5,7},{7,5},{8,10},{10,8},{9,1... | collective-permute-start | bytes 3145736 | tf_op jit(solution)/shard_map/ppermute | solution.py:488
  44.9 11.1 %collective-permute-start.6 = (bf16[512,640]{1,0:T(8,128)(2,1)S(1)}, bf16[512,640]{1,0:T(8,128)(2,1)S(1)}, u32[]{:S(2)}, u32[]{:S(2)}) collective-permute-start(bf16[512,640]{1,0:T(8,128)(2,1)S(1)} %near.1.rest_0_.mine), channel_id=1, source_target_pairs={{0,1},{1,0},{2,3},{3,2},{4,5},{5,4},{6,7},{7,6},{8,9},{9,8},{10,11... | collective-permute-start | bytes 1966088 | tf_op jit(solution)/shard_map/ppermute | solution.py:485
  56.0 4.4 %collective-permute-start.10 = (bf16[512,640]{1,0:T(8,128)(2,1)S(1)}, bf16[512,640]{1,0:T(8,128)(2,1)S(1)}, u32[]{:S(2)}, u32[]{:S(2)}) collective-permute-start(bf16[512,640]{1,0:T(8,128)(2,1)S(1)} %gate.1.rest_0_.refs_1_.mine), channel_id=1, source_target_pairs={{0,1},{1,0},{2,3},{3,2},{4,5},{5,4},{6,7},{7,6},{8,9},{9,8},{10,11... | collective-permute-start | bytes 1966088 | tf_op jit(solution)/shard_map/ppermute | solution.py:490
where the time goes:
time: 79.2 us; the launch traced here: 79 us
  waiting for transfers between devices  35.2 us (44%)
  Pallas kernels  34.7 us (44%)
  starting transfers between devices  9.04 us (11%)
    pallas_call x1, Pallas kernels, attend_current(): pl.pallas_call(functools.partial(current_kernel, 512), in_specs=[HBM] * 3...  11.3 us
    ppermute x3, waiting for transfers between devices, local(): lax.ppermute(sent, 'seq', [(index, index ^ flip) for index in range(seq_c...  11.2 us
    ppermute x1, waiting for transfers between devices, local(): came_mine = lax.ppermute(far, 'head', SWAP)  11.1 us
    ppermute x1, waiting for transfers between devices, local(): group_columns = lax.ppermute(columns, 'groups', SWAP)  8.6 us
    pallas_call x4, Pallas kernels, finish_block(): pl.pallas_call(body, in_specs=[VMEM] * count + [HBM] * len(totals), out_s...  6.16 us
    pallas_call x2, Pallas kernels, project_call(): pl.pallas_call(kernel, in_specs=[VMEM] * 3 + [ANY] * len(after), out_spec...  5.94 us
    pallas_call x3, Pallas kernels, attend_frames(): pl.pallas_call(functools.partial(frames_kernel, heads, half, state_half,...  4.93 us
    ppermute x3, starting transfers between devices, local(): lax.ppermute(sent, 'seq', [(index, index ^ flip) for index in range(seq_c...  4.45 us
  transfers between devices with their start and end apart: 13, of which 6 were waited for; matrix products, arithmetic and copies ran while one was open for 0% of the time, Pallas kernels for 39%

commit v1 on v0

--- a/solution.py
+++ b/solution.py
@@ -196,18 +196,18 @@
     )(in_vmem(array), in_vmem(after))
 
 
-def copied_kernel(array, after, out):
-    out[...] = array[...]
-
-
-def copied(array, after):
-    return pl.pallas_call(
-        copied_kernel,
+def leading_kernel(array, after, out):
+    out[...] = array[:, pl.ds(0, out.shape[1])]
+
+
+def leading(array, width, after):
+    return pl.pallas_call(
+        leading_kernel,
         in_specs=[VMEM, ANY],
         out_specs=VMEM,
-        out_shape=pltpu.VMEM(array.shape, array.dtype),
-        compiler_params=params(),
-        name="copied",
+        out_shape=pltpu.VMEM((array.shape[0], width), array.dtype),
+        compiler_params=params(),
+        name="leading",
         cost_estimate=SHORT,
     )(in_vmem(array), in_vmem(after))
 
@@ -261,7 +261,7 @@
         compiler_params=params(),
         name="attend_current",
         cost_estimate=pl.CostEstimate(
-            flops=60 * heads * rows * 2 * keys * HD, bytes_accessed=heads * rows * HD * 12, transcendentals=heads * rows * 2 * keys
+            flops=6 * heads * rows * 2 * keys * HD, bytes_accessed=heads * rows * HD * 12, transcendentals=heads * rows * 2 * keys
         ),
     )(in_hbm(queries), in_hbm(cur_keys), in_hbm(cur_values), in_vmem(sibling))
 
@@ -356,15 +356,20 @@
         out[:, columns] = jnp.dot(rows, weight[:, columns], preferred_element_type=F32).astype(BF16)
 
 
-def unshared_columns(low, share):
-    return pl.ds(0, low), pl.ds(pl.multiple_of(low + quarter(True, True) * share, 128), share)
-
-
-def unshared_kernel(low, mine, other, weight, *rest):
+def unshared_columns(low, share, passed):
+    found = [pl.ds(0, low)] if low else []
+    for other_seq, other_group, skipped in ((True, True, 0), (False, True, passed), (True, False, passed)):
+        if skipped < share:
+            start = low + quarter(other_seq, other_group) * share + skipped
+            found.append(pl.ds(pl.multiple_of(start, 128), share - skipped))
+    return found
+
+
+def unshared_kernel(low, share, passed, mine, other, weight, *rest):
     out = rest[-1]
     rows = both(mine, other)
     start = 0
-    for columns in unshared_columns(low, out.shape[1] - low):
+    for columns in unshared_columns(low, share, passed):
         out[:, pl.ds(start, columns.size)] = jnp.dot(rows, weight[:, columns], preferred_element_type=F32).astype(BF16)
         start += columns.size
 
@@ -385,9 +390,10 @@
     return project_call(functools.partial(project_kernel, 512), "project", mine, other, weight, weight.shape[1], after)
 
 
-def project_unshared(mine, other, weight, low, share, after):
-    kernel = functools.partial(unshared_kernel, low)
-    return project_call(kernel, "project_unshared", mine, other, weight, low + share, after)
+def project_unshared(mine, other, weight, low, share, passed, after):
+    kernel = functools.partial(unshared_kernel, low, share, passed)
+    width = low + share + 2 * (share - passed)
+    return project_call(kernel, "project_unshared", mine, other, weight, width, after)
 
 
 def write_blocks(blocks, out, scratch, sems):
@@ -403,16 +409,16 @@
         copy.wait()
 
 
-def remote_kernel(first, other_seq, other_group, terms, mine, other, weight, total, out, scratch, sems):
+def remote_kernel(first, share, other_seq, other_group, terms, mine, other, weight, total, out, scratch, sems):
     block = weight.shape[1]
-    low = pl.multiple_of(first + quarter(other_seq, other_group) * block, 128)
+    low = pl.multiple_of(first + quarter(other_seq, other_group) * share, 128)
     product = jnp.dot(both(mine, other), weight[...], preferred_element_type=F32)
     write_blocks([(terms[:, pl.ds(low, block)].astype(F32) + product, low)], out, scratch, sems)
 
 
-def add_kernel(low, terms, came, total, out, scratch, sems):
+def add_kernel(low, share, passed, terms, came, total, out, scratch, sems):
     blocks, start = [], 0
-    for columns in unshared_columns(low, came.shape[1] - low):
+    for columns in unshared_columns(low, share, passed):
         block = terms[:, columns].astype(F32) + came[:, pl.ds(start, columns.size)].astype(F32)
         blocks.append((block, columns.start))
         start += columns.size
@@ -432,20 +438,20 @@
         out_specs=HBM,
         out_shape=pltpu.HBM((rows, width), BF16),
         input_output_aliases=aliases,
-        scratch_shapes=[pltpu.VMEM((rows, block), BF16), pltpu.SemaphoreType.DMA((2,))],
+        scratch_shapes=[pltpu.VMEM((rows, block), BF16), pltpu.SemaphoreType.DMA((4,))],
         compiler_params=params(),
         name=name,
         cost_estimate=SHORT,
     )(*map(in_vmem, operands), *totals)
 
 
-def add_remote(terms, mine, other, weight, first, other_seq, other_group, total):
-    kernel = functools.partial(remote_kernel, first, other_seq, other_group)
+def add_remote(terms, mine, other, weight, first, share, other_seq, other_group, total):
+    kernel = functools.partial(remote_kernel, first, share, other_seq, other_group)
     return finish_block(kernel, "add_remote", (terms, mine, other, weight), total, *terms.shape, weight.shape[1])
 
 
-def add_unshared(terms, came, low, total):
-    kernel = functools.partial(add_kernel, low)
+def add_unshared(terms, came, low, share, passed, total):
+    kernel = functools.partial(add_kernel, low, share, passed)
     return finish_block(kernel, "add_unshared", (terms, came), total, *terms.shape, came.shape[1])
 
 
@@ -454,7 +460,8 @@
     heads = queries.shape[1] // HD // 2
     keys = cur_keys.shape[0]
     out_cols = out_weight.shape[1]
-    share = out_cols // 5 // 128 * 128
+    share = out_cols // 4 // 128 * 128
+    passed_on = share * 4 // 5 // 128 * 128
     low = out_cols - 4 * share
 
     *sends, to_sibling, columns = pack(
@@ -477,24 +484,24 @@
     far = attend_frames("far_last", far_half, bias, seq_count, q, *state, others, starts, True)
     came_mine = lax.ppermute(far, "head", SWAP)
     far_sibling = lax.ppermute(far, "sub", SWAP)
-    group_columns = lax.ppermute(columns, "groups", SWAP)
-    columns_copy = copied(columns, far)
+    columns_copy = leading(columns, passed_on, far)
+    group_columns = lax.ppermute(columns_copy, "groups", SWAP)
     seq_columns = lax.ppermute(columns_copy, "seq", [(index, index ^ 1) for index in range(seq_count)])
     starts = [0] * seq_count + starts
     near = attend_frames("near", near_half, bias, 0, q, held, lse, mine + others, starts, True, (columns_copy,))
     near_sibling = lax.ppermute(near, "sub", SWAP)
 
-    term = project_unshared(far, far_sibling, weight, low, share, (near,))
+    term = project_unshared(far, far_sibling, weight, low, share, passed_on, (near,))
     came = lax.ppermute(term, "head", SWAP)
     came_mine = gate(came_mine, term)
     came_other = lax.ppermute(came_mine, "sub", SWAP)
     terms = project(near, near_sibling, weight, (came_mine,))
 
     arrived = (terms, came_mine, came_other)
-    total = add_remote(*arrived, columns, low, False, False, None)
-    total = add_remote(*arrived, group_columns, low, False, True, total)
-    total = add_remote(*arrived, seq_columns, low, True, False, total)
-    return add_unshared(terms, came, low, total)
+    total = add_remote(*arrived, columns, low, share, False, False, None)
+    total = add_remote(*arrived, group_columns, low, share, False, True, total)
+    total = add_remote(*arrived, seq_columns, low, share, True, False, total)
+    return add_unshared(terms, came, low, share, passed_on, total)
 
 
 def local_any(queries, cur_keys, cur_values, mem_keys, mem_values, frame_ids, frame_counts, out_weight):

time: 79.2 us -> 77.7 us (0.981)
  the two profiles are of different devices: /device:TPU:20 before, /device:TPU:0 now
where the time goes in v1:
time: 77.7 us; the launch traced here: 77.4 us
  Pallas kernels  35.5 us (46%)
  waiting for transfers between devices  28.9 us (37%)
  starting transfers between devices  12.9 us (17%)
    pallas_call x1, Pallas kernels, attend_current(): pl.pallas_call(functools.partial(current_kernel, 512), in_specs=[HBM] * 3...  11.3 us
    ppermute x1, waiting for transfers between devices, local(): group_columns = lax.ppermute(columns_copy, 'groups', SWAP)  9.88 us
    ppermute x3, waiting for transfers between devices, local(): lax.ppermute(sent, 'seq', [(index, index ^ flip) for index in range(seq_c...  6.97 us
    pallas_call x4, Pallas kernels, finish_block(): pl.pallas_call(body, in_specs=[VMEM] * count + [HBM] * len(totals), out_s...  6.61 us
    ppermute x1, waiting for transfers between devices, local(): columns = lax.ppermute(columns, 'head', SWAP)  6.5 us
    pallas_call x2, Pallas kernels, project_call(): pl.pallas_call(kernel, in_specs=[VMEM] * 3 + [ANY] * len(after), out_spec...  6.28 us
    ppermute x1, waiting for transfers between devices, local(): came_mine = lax.ppermute(far, 'head', SWAP)  5.11 us
    pallas_call x3, Pallas kernels, attend_frames(): pl.pallas_call(functools.partial(frames_kernel, heads, half, state_half,...  4.89 us
  transfers between devices with their start and end apart: 13, of which 6 were waited for; matrix products, arithmetic and copies ran while one was open for 0% of the time, Pallas kernels for 41%

profile of v1, /device:TPU:0, one launch (start us, length us, event | category | flops | bytes accessed | tf_op | source)
XLA Modules:
  0.0 77.4 jit_solution(16274162225472139391)
XLA Ops:
  0.0 2.7 %pack.1 = (bf16[128,640]{1,0:T(8,128)(2,1)S(1)}, bf16[256,640]{1,0:T(8,128)(2,1)S(1)}, bf16[256,640]{1,0:T(8,128)(2,1)S(1)}, bf16[256,640]{1,0:T(8,128)(2,1)S(1)...) custom-call(s32[4,8]{1,0:T(4,128)} %ids.1, bf16[16,64,1280]{2,1,0:T(8,128)(2,1)} %keys.1, ...), custom_call_target="tpu_custom_call" | custom-call | bytes 12582912 | tf_op jit(solution)/shard_map/pack/pallas_call | solution.py:118
  2.7 0.5 collective-permute-start
  3.2 2.6 %collective-permute-start.5 = (bf16[1280,640]{1,0:T(8,128)(2,1)S(1)}, bf16[1280,640]{1,0:T(8,128)(2,1)S(1)}, u32[]{:S(2)}, u32[]{:S(2)}) collective-permute-start(bf16[1280,640]{1,0:T(8,128)(2,1)S(1)} %get-tuple-element.28), channel_id=1, source_target_pairs={{0,2},{2,0},{1,3},{3,1},{4,6},{6,4},{5,7},{7,5},{8,10},{10,8},{9,1... | collective-permute-start | bytes 4915208 | tf_op jit(solution)/shard_map/ppermute | solution.py:473
  5.8 2.6 %collective-permute-start.1 = (bf16[256,640]{1,0:T(8,128)(2,1)S(1)}, bf16[256,640]{1,0:T(8,128)(2,1)S(1)}, u32[]{:S(2)}, u32[]{:S(2)}) collective-permute-start(bf16[256,640]{1,0:T(8,128)(2,1)S(1)} %get-tuple-element.24), channel_id=1, source_target_pairs={{0,8},{4,12},{8,0},{12,4},{1,9},{5,13},{9,1},{13,5},{2,10},{6,14},... | collective-permute-start | bytes 983048 | tf_op jit(solution)/shard_map/ppermute | solution.py:472
  8.4 1.3 %collective-permute-start.2 = (bf16[256,640]{1,0:T(8,128)(2,1)S(1)}, bf16[256,640]{1,0:T(8,128)(2,1)S(1)}, u32[]{:S(2)}, u32[]{:S(2)}) collective-permute-start(bf16[256,640]{1,0:T(8,128)(2,1)S(1)} %get-tuple-element.25), channel_id=1, source_target_pairs={{0,12},{4,8},{8,4},{12,0},{1,13},{5,9},{9,5},{13,1},{2,14},{6,10},... | collective-permute-start | bytes 983048 | tf_op jit(solution)/shard_map/ppermute | solution.py:472
  10.0 11.3 %attend_current.1 = (f32[5,1024,128]{2,1,0:T(8,128)S(1)}, f32[5,1024,128]{2,1,0:T(8,128)S(1)}, bf16[1024,640]{1,0:T(8,128)(2,1)S(1)}) custom-call(bf16[1024,1280]{1,0:T(8,128)(2,1)} %queries.1, bf16[512,1280]{1,0:T(8,128)(2,1)} %own_keys.1, bf16[512,1280]{1,0:T(8,128)(2,1)} %own_values.1, bf16[1152,640]{1,0:T(8,128)(2,1)S(1)} %collective-permute-done.sibling.rest_0_.rest_4_), custom_call_target="tpu_custom_call" | custom-call | flops 4026531840 | bytes 7864320 | tf_op jit(solution)/shard_map/attend_current/pallas_call | solution.py:255
  21.3 3.6 %load.1 = (bf16[1280,2560]{1,0:T(8,128)(2,1)S(1)}, f32[8,64]{1,0:T(8,128)S(1)}) custom-call(s32[4,8]{1,0:T(4,128)} %ids.1, s32[128]{0:T(128)} %counts.1, bf16[1280,2560]{1,0:T(8,128)(2,1)} %weight.3, f32[5,1024,128]{2,1,0:T(8,128)S(1)} %get-tuple-element.19.after.lse), custom_call_target="tpu_custom_call" | custom-call | bytes 6553600 | tf_op jit(solution)/shard_map/load/pallas_call | solution.py:174
  24.9 6.4 %collective-permute-done.1.refs_0_.rest_1_ = bf16[256,640]{1,0:T(8,128)(2,1)S(1)} collective-permute-done((bf16[256,640]{1,0:T(8,128)(2,1)S(1)}, bf16[256,640]{1,0:T(8,128)(2,1)S(1)}, u32[]{:S(2)}, u32[]{:S(2)}) %collective-permute-start.1) | collective-permute-done | bytes 327712 | tf_op jit(solution)/shard_map/ppermute | solution.py:472
  31.3 0.5 collective-permute-done.3.refs_2_.rest_3_
  32.0 1.4 %far_first.1 = (f32[5,512,128]{2,1,0:T(8,128)S(1)}, f32[5,512,128]{2,1,0:T(8,128)S(1)}) custom-call(f32[8,64]{1,0:T(8,128)S(1)} %get-tuple-element.20.bias, bf16[1024,640]{1,0:T(8,128)(2,1)S(1)} %get-tuple-element.21.q, f32[5,1024,128]{2,1,0:T(8,128)S(1)} %get-tuple-element.22.held, f32[5,1024,128]{2,1,0:T(8,128)S(1)} %get-tuple-element.19.after.lse, ...), custom_call_target="tpu_custom_call" | custom-call | flops 1024 | bytes 1024 | tf_op jit(solution)/shard_map/far_first/pallas_call | solution.py:328
  33.9 1.4 %far_last.1.after.mine = bf16[512,640]{1,0:T(8,128)(2,1)S(1)} custom-call(f32[8,64]{1,0:T(8,128)S(1)} %get-tuple-element.20.bias, bf16[1024,640]{1,0:T(8,128)(2,1)S(1)} %get-tuple-element.21.q, f32[5,512,128]{2,1,0:T(8,128)S(1)} %get-tuple-element.29.held, f32[5,512,128]{2,1,0:T(8,128)S(1)} %get-tuple-element.30.lse, ...), custom_call_target="tpu_custom_call" | custom-call | flops 1024 | bytes 1024 | tf_op jit(solution)/shard_map/far_last/pallas_call | solution.py:328
  36.0 6.5 %collective-permute-done.5.array.refs_3_ = bf16[1280,640]{1,0:T(8,128)(2,1)S(1)} collective-permute-done((bf16[1280,640]{1,0:T(8,128)(2,1)S(1)}, bf16[1280,640]{1,0:T(8,128)(2,1)S(1)}, u32[]{:S(2)}, u32[]{:S(2)}) %collective-permute-start.5) | collective-permute-done | bytes 1638432 | tf_op jit(solution)/shard_map/ppermute | solution.py:473
  42.5 2.0 %collective-permute-start.12 = (bf16[1280,512]{1,0:T(8,128)(2,1)S(1)}, bf16[1280,512]{1,0:T(8,128)(2,1)S(1)}, u32[]{:S(2)}, u32[]{:S(2)}) collective-permute-start(bf16[1280,512]{1,0:T(8,128)(2,1)S(1)} %leading.1.rest_8_), channel_id=1, source_target_pairs={{0,16},{16,0},{1,17},{17,1},{2,18},{18,2},{3,19},{19,3},{4,20},{20... | collective-permute-start | bytes 3932168 | tf_op jit(solution)/shard_map/ppermute | solution.py:488
  44.6 1.1 %collective-permute-start.11 = (bf16[1280,512]{1,0:T(8,128)(2,1)S(1)}, bf16[1280,512]{1,0:T(8,128)(2,1)S(1)}, u32[]{:S(2)}, u32[]{:S(2)}) collective-permute-start(bf16[1280,512]{1,0:T(8,128)(2,1)S(1)} %leading.1.rest_8_), channel_id=1, source_target_pairs={{0,4},{4,0},{8,12},{12,8},{1,5},{5,1},{9,13},{13,9},{2,6},{6,2},{1... | collective-permute-start | bytes 3932168 | tf_op jit(solution)/shard_map/ppermute | solution.py:489
  45.7 2.1 %near.1.rest_0_.mine = bf16[512,640]{1,0:T(8,128)(2,1)S(1)} custom-call(f32[8,64]{1,0:T(8,128)S(1)} %get-tuple-element.20.bias, bf16[1024,640]{1,0:T(8,128)(2,1)S(1)} %get-tuple-element.21.q, f32[5,1024,128]{2,1,0:T(8,128)S(1)} %get-tuple-element.22.held, f32[5,1024,128]{2,1,0:T(8,128)S(1)} %get-tuple-element.19.after.lse, ...), custom_call_target="tpu_custom_call" | custom-call | flops 1024 | bytes 1024 | tf_op jit(solution)/shard_map/near/pallas_call | solution.py:328
  47.8 1.9 %project_unshared.1.refs_1_ = bf16[512,896]{1,0:T(8,128)(2,1)S(1)} custom-call(bf16[512,640]{1,0:T(8,128)(2,1)S(1)} %far_last.1.after.mine, bf16[512,640]{1,0:T(8,128)(2,1)S(1)} %collective-permute-done.8.other, bf16[1280,2560]{1,0:T(8,128)(2,1)S(1)} %get-tuple-element.27.refs_3_.weight, bf16[512,640]{1,0:T(8,128)(2,1)S(1)} %near.1.rest_0_.mine), custom_call_target="tpu_custom_call" | custom-call | flops 1024 | bytes 1024 | tf_op jit(solution)/shard_map/project_unshared/pallas_call | solution.py:378
  49.7 1.7 %collective-permute-start.9 = (bf16[512,896]{1,0:T(8,128)(2,1)S(1)}, bf16[512,896]{1,0:T(8,128)(2,1)S(1)}, u32[]{:S(2)}, u32[]{:S(2)}) collective-permute-start(bf16[512,896]{1,0:T(8,128)(2,1)S(1)} %project_unshared.1.refs_1_), channel_id=1, source_target_pairs={{0,2},{2,0},{1,3},{3,1},{4,6},{6,4},{5,7},{7,5},{8,10},{10,8},{9,1... | collective-permute-start | bytes 2752520 | tf_op jit(solution)/shard_map/ppermute | solution.py:495
  51.4 5.1 %collective-permute-done.7.refs_0_ = bf16[512,640]{1,0:T(8,128)(2,1)S(1)} collective-permute-done((bf16[512,640]{1,0:T(8,128)(2,1)S(1)}, bf16[512,640]{1,0:T(8,128)(2,1)S(1)}, u32[]{:S(2)}, u32[]{:S(2)}) %collective-permute-start.7) | collective-permute-done | bytes 655392 | tf_op jit(solution)/shard_map/ppermute | solution.py:485
  56.5 4.4 %project.1.refs_0_.terms = bf16[512,2560]{1,0:T(8,128)(2,1)S(1)} custom-call(bf16[512,640]{1,0:T(8,128)(2,1)S(1)} %near.1.rest_0_.mine, bf16[512,640]{1,0:T(8,128)(2,1)S(1)} %collective-permute-done.6.other, bf16[1280,2560]{1,0:T(8,128)(2,1)S(1)} %get-tuple-element.27.refs_3_.weight, bf16[512,640]{1,0:T(8,128)(2,1)S(1)} %gate.1.rest_0_.refs_1_.mine), custom_call_target="tpu_custom_call" | custom-call | flops 1024 | bytes 1024 | tf_op jit(solution)/shard_map/project/pallas_call | solution.py:378
  60.9 2.1 %add_remote.3.total = bf16[512,2560]{1,0:T(8,128)(2,1)} custom-call(bf16[512,2560]{1,0:T(8,128)(2,1)S(1)} %project.1.refs_0_.terms, bf16[512,640]{1,0:T(8,128)(2,1)S(1)} %gate.1.rest_0_.refs_1_.mine, bf16[512,640]{1,0:T(8,128)(2,1)S(1)} %collective-permute-done.10.refs_2_.other, bf16[1280,640]{1,0:T(8,128)(2,1)S(1)} %collective-permute-done.5.array.refs_3_), custom_call_target="tpu_custom_call" | custom-call | flops 1024 | bytes 1024 | tf_op jit(solution)/shard_map/add_remote/pallas_call | solution.py:435
  63.0 9.9 %collective-permute-done.12.weight = bf16[1280,512]{1,0:T(8,128)(2,1)S(1)} collective-permute-done((bf16[1280,512]{1,0:T(8,128)(2,1)S(1)}, bf16[1280,512]{1,0:T(8,128)(2,1)S(1)}, u32[]{:S(2)}, u32[]{:S(2)}) %collective-permute-start.12) | collective-permute-done | bytes 1310752 | tf_op jit(solution)/shard_map/ppermute | solution.py:488
  72.9 1.7 %add_remote.4.total = bf16[512,2560]{1,0:T(8,128)(2,1)} custom-call(bf16[512,2560]{1,0:T(8,128)(2,1)S(1)} %project.1.refs_0_.terms, bf16[512,640]{1,0:T(8,128)(2,1)S(1)} %gate.1.rest_0_.refs_1_.mine, bf16[512,640]{1,0:T(8,128)(2,1)S(1)} %collective-permute-done.10.refs_2_.other, ...), custom_call_target="tpu_custom_call", output_to_operand_aliasing={{}: (4, {})} | custom-call | flops 1024 | bytes 1024 | tf_op jit(solution)/shard_map/add_remote/pallas_call | solution.py:435
  74.6 1.7 %add_remote.5.total = bf16[512,2560]{1,0:T(8,128)(2,1)} custom-call(bf16[512,2560]{1,0:T(8,128)(2,1)S(1)} %project.1.refs_0_.terms, bf16[512,640]{1,0:T(8,128)(2,1)S(1)} %gate.1.rest_0_.refs_1_.mine, bf16[512,640]{1,0:T(8,128)(2,1)S(1)} %collective-permute-done.10.refs_2_.other, ...), custom_call_target="tpu_custom_call", output_to_operand_aliasing={{}: (4, {})} | custom-call | flops 1024 | bytes 1024 | tf_op jit(solution)/shard_map/add_remote/pallas_call | solution.py:435
  76.3 1.1 %add_unshared.1 = bf16[512,2560]{1,0:T(8,128)(2,1)} custom-call(bf16[512,2560]{1,0:T(8,128)(2,1)S(1)} %project.1.refs_0_.terms, bf16[512,896]{1,0:T(8,128)(2,1)S(1)} %collective-permute-done.9.came, bf16[512,2560]{1,0:T(8,128)(2,1)} %add_remote.5.total), custom_call_target="tpu_custom_call", output_to_operand_aliasing={{}: (2, {})} | custom-call | flops 1024 | bytes 1024 | tf_op jit(solution)/shard_map/add_unshared/pallas_call | solution.py:435
  (17 shorter events, 1.6 us)
Async XLA Ops:
  2.7 7.3 %collective-permute-start = (bf16[1152,640]{1,0:T(8,128)(2,1)S(1)}, bf16[1152,640]{1,0:T(8,128)(2,1)S(1)}, u32[]{:S(2)}, u32[]{:S(2)}) collective-permute-start(bf16[1152,640]{1,0:T(8,128)(2,1)S(1)} %get-tuple-element.18), channel_id=1, source_target_pairs={{0,1},{1,0},{2,3},{3,2},{4,5},{5,4},{6,7},{7,6},{8,9},{9,8},{10,11... | collective-permute-start | bytes 4423688 | tf_op jit(solution)/shard_map/ppermute | solution.py:474
  3.2 39.2 %collective-permute-start.5 = (bf16[1280,640]{1,0:T(8,128)(2,1)S(1)}, bf16[1280,640]{1,0:T(8,128)(2,1)S(1)}, u32[]{:S(2)}, u32[]{:S(2)}) collective-permute-start(bf16[1280,640]{1,0:T(8,128)(2,1)S(1)} %get-tuple-element.28), channel_id=1, source_target_pairs={{0,2},{2,0},{1,3},{3,1},{4,6},{6,4},{5,7},{7,5},{8,10},{10,8},{9,1... | collective-permute-start | bytes 4915208 | tf_op jit(solution)/shard_map/ppermute | solution.py:473
  5.8 25.5 %collective-permute-start.1 = (bf16[256,640]{1,0:T(8,128)(2,1)S(1)}, bf16[256,640]{1,0:T(8,128)(2,1)S(1)}, u32[]{:S(2)}, u32[]{:S(2)}) collective-permute-start(bf16[256,640]{1,0:T(8,128)(2,1)S(1)} %get-tuple-element.24), channel_id=1, source_target_pairs={{0,8},{4,12},{8,0},{12,4},{1,9},{5,13},{9,1},{13,5},{2,10},{6,14},... | collective-permute-start | bytes 983048 | tf_op jit(solution)/shard_map/ppermute | solution.py:472
  8.4 23.0 %collective-permute-start.2 = (bf16[256,640]{1,0:T(8,128)(2,1)S(1)}, bf16[256,640]{1,0:T(8,128)(2,1)S(1)}, u32[]{:S(2)}, u32[]{:S(2)}) collective-permute-start(bf16[256,640]{1,0:T(8,128)(2,1)S(1)} %get-tuple-element.25), channel_id=1, source_target_pairs={{0,12},{4,8},{8,4},{12,0},{1,13},{5,9},{9,5},{13,1},{2,14},{6,10},... | collective-permute-start | bytes 983048 | tf_op jit(solution)/shard_map/ppermute | solution.py:472
  9.7 22.2 %collective-permute-start.3 = (bf16[256,640]{1,0:T(8,128)(2,1)S(1)}, bf16[256,640]{1,0:T(8,128)(2,1)S(1)}, u32[]{:S(2)}, u32[]{:S(2)}) collective-permute-start(bf16[256,640]{1,0:T(8,128)(2,1)S(1)} %get-tuple-element.26), channel_id=1, source_target_pairs={{0,4},{4,0},{8,12},{12,8},{1,5},{5,1},{9,13},{13,9},{2,6},{6,2},{1... | collective-permute-start | bytes 983048 | tf_op jit(solution)/shard_map/ppermute | solution.py:472
  31.9 1.9 %collective-permute-start.4 = (bf16[384,640]{1,0:T(8,128)(2,1)S(1)}, bf16[384,640]{1,0:T(8,128)(2,1)S(1)}, u32[]{:S(2)}, u32[]{:S(2)}) collective-permute-start(bf16[384,640]{1,0:T(8,128)(2,1)S(1)} %pass_on.1.rest_4_), channel_id=1, source_target_pairs={{0,1},{1,0},{2,3},{3,2},{4,5},{5,4},{6,7},{7,6},{8,9},{9,8},{10,11... | collective-permute-start | bytes 1474568 | tf_op jit(solution)/shard_map/ppermute | solution.py:479
  35.2 12.5 %collective-permute-start.8 = (bf16[512,640]{1,0:T(8,128)(2,1)S(1)}, bf16[512,640]{1,0:T(8,128)(2,1)S(1)}, u32[]{:S(2)}, u32[]{:S(2)}) collective-permute-start(bf16[512,640]{1,0:T(8,128)(2,1)S(1)} %far_last.1.after.mine), channel_id=1, source_target_pairs={{0,1},{1,0},{2,3},{3,2},{4,5},{5,4},{6,7},{7,6},{8,9},{9,8},{10,11... | collective-permute-start | bytes 1966088 | tf_op jit(solution)/shard_map/ppermute | solution.py:486
  35.5 21.0 %collective-permute-start.7 = (bf16[512,640]{1,0:T(8,128)(2,1)S(1)}, bf16[512,640]{1,0:T(8,128)(2,1)S(1)}, u32[]{:S(2)}, u32[]{:S(2)}) collective-permute-start(bf16[512,640]{1,0:T(8,128)(2,1)S(1)} %far_last.1.after.mine), channel_id=1, source_target_pairs={{0,2},{2,0},{1,3},{3,1},{4,6},{6,4},{5,7},{7,5},{8,10},{10,8},{9,1... | collective-permute-start | bytes 1966088 | tf_op jit(solution)/shard_map/ppermute | solution.py:485
  42.5 30.3 %collective-permute-start.12 = (bf16[1280,512]{1,0:T(8,128)(2,1)S(1)}, bf16[1280,512]{1,0:T(8,128)(2,1)S(1)}, u32[]{:S(2)}, u32[]{:S(2)}) collective-permute-start(bf16[1280,512]{1,0:T(8,128)(2,1)S(1)} %leading.1.rest_8_), channel_id=1, source_target_pairs={{0,16},{16,0},{1,17},{17,1},{2,18},{18,2},{3,19},{19,3},{4,20},{20... | collective-permute-start | bytes 3932168 | tf_op jit(solution)/shard_map/ppermute | solution.py:488
  44.6 30.0 %collective-permute-start.11 = (bf16[1280,512]{1,0:T(8,128)(2,1)S(1)}, bf16[1280,512]{1,0:T(8,128)(2,1)S(1)}, u32[]{:S(2)}, u32[]{:S(2)}) collective-permute-start(bf16[1280,512]{1,0:T(8,128)(2,1)S(1)} %leading.1.rest_8_), channel_id=1, source_target_pairs={{0,4},{4,0},{8,12},{12,8},{1,5},{5,1},{9,13},{13,9},{2,6},{6,2},{1... | collective-permute-start | bytes 3932168 | tf_op jit(solution)/shard_map/ppermute | solution.py:489
  49.7 26.6 %collective-permute-start.9 = (bf16[512,896]{1,0:T(8,128)(2,1)S(1)}, bf16[512,896]{1,0:T(8,128)(2,1)S(1)}, u32[]{:S(2)}, u32[]{:S(2)}) collective-permute-start(bf16[512,896]{1,0:T(8,128)(2,1)S(1)} %project_unshared.1.refs_1_), channel_id=1, source_target_pairs={{0,2},{2,0},{1,3},{3,1},{4,6},{6,4},{5,7},{7,5},{8,10},{10,8},{9,1... | collective-permute-start | bytes 2752520 | tf_op jit(solution)/shard_map/ppermute | solution.py:495
  51.4 5.1 %collective-permute-start.6 = (bf16[512,640]{1,0:T(8,128)(2,1)S(1)}, bf16[512,640]{1,0:T(8,128)(2,1)S(1)}, u32[]{:S(2)}, u32[]{:S(2)}) collective-permute-start(bf16[512,640]{1,0:T(8,128)(2,1)S(1)} %near.1.rest_0_.mine), channel_id=1, source_target_pairs={{0,1},{1,0},{2,3},{3,2},{4,5},{5,4},{6,7},{7,6},{8,9},{9,8},{10,11... | collective-permute-start | bytes 1966088 | tf_op jit(solution)/shard_map/ppermute | solution.py:492
  56.5 4.4 %collective-permute-start.10 = (bf16[512,640]{1,0:T(8,128)(2,1)S(1)}, bf16[512,640]{1,0:T(8,128)(2,1)S(1)}, u32[]{:S(2)}, u32[]{:S(2)}) collective-permute-start(bf16[512,640]{1,0:T(8,128)(2,1)S(1)} %gate.1.rest_0_.refs_1_.mine), channel_id=1, source_target_pairs={{0,1},{1,0},{2,3},{3,2},{4,5},{5,4},{6,7},{7,6},{8,9},{9,8},{10,11... | collective-permute-start | bytes 1966088 | tf_op jit(solution)/shard_map/ppermute | solution.py:497

commit v2 on v1

--- a/solution.py
+++ b/solution.py
@@ -50,7 +50,7 @@
 
 
 def exchange_order(seq_count):
-    return [0, *range(seq_count // 2, seq_count), *range(1, seq_count // 2)]
+    return [0, *range(seq_count - 1, 0, -1)]
 
 
 def held_by(ids, stretch, owner, count):

time: 77.7 us -> 79.3 us (1.021)
  starting transfers between devices: 12.9 us -> 13.7 us
    ppermute x1, waiting for transfers between devices: 6.5 us -> 0.41 us  [local(): columns = lax.ppermute(columns, 'head', SWAP)]
    ppermute x3, waiting for transfers between devices: 6.97 us -> 12.5 us  [local(): lax.ppermute(sent, 'seq', [(index, index ^ flip) for index in range(seq_c...]
    ppermute x1, waiting for transfers between devices: 9.88 us -> 7.58 us  [local(): group_columns = lax.ppermute(columns_copy, 'groups', SWAP)]
    ppermute x1, waiting for transfers between devices: 5.11 us -> 7.07 us  [local(): came_mine = lax.ppermute(far, 'head', SWAP)]
    ppermute x1, waiting for transfers between devices: 0.01 us -> 1.62 us  [local(): came = lax.ppermute(term, 'head', SWAP)]
  transfers between devices with their start and end apart: 13 -> 13, of which waited for: 6 -> 6; matrix products, arithmetic and copies ran while one was open for 0% -> 0% of each run, Pallas kernels for 41% -> 40%
where the time goes in v2:
time: 79.3 us; the launch traced here: 79 us
  Pallas kernels  35.5 us (45%)
  waiting for transfers between devices  29.6 us (37%)
  starting transfers between devices  13.7 us (17%)
    ppermute x3, waiting for transfers between devices, local(): lax.ppermute(sent, 'seq', [(index, index ^ flip) for index in range(seq_c...  12.5 us
    pallas_call x1, Pallas kernels, attend_current(): pl.pallas_call(functools.partial(current_kernel, 512), in_specs=[HBM] * 3...  11.3 us
    ppermute x1, waiting for transfers between devices, local(): group_columns = lax.ppermute(columns_copy, 'groups', SWAP)  7.58 us
    ppermute x1, waiting for transfers between devices, local(): came_mine = lax.ppermute(far, 'head', SWAP)  7.07 us
    pallas_call x4, Pallas kernels, finish_block(): pl.pallas_call(body, in_specs=[VMEM] * count + [HBM] * len(totals), out_s...  6.6 us
    pallas_call x2, Pallas kernels, project_call(): pl.pallas_call(kernel, in_specs=[VMEM] * 3 + [ANY] * len(after), out_spec...  6.28 us
    pallas_call x3, Pallas kernels, attend_frames(): pl.pallas_call(functools.partial(frames_kernel, heads, half, state_half,...  4.89 us
    ppermute x3, starting transfers between devices, local(): lax.ppermute(sent, 'seq', [(index, index ^ flip) for index in range(seq_c...  4.39 us
  transfers between devices with their start and end apart: 13, of which 6 were waited for; matrix products, arithmetic and copies ran while one was open for 0% of the time, Pallas kernels for 40%

profile of v2, /device:TPU:0, one launch (start us, length us, event | category | flops | bytes accessed | tf_op | source)
XLA Modules:
  0.0 79.0 jit_solution(12811091394709229405)
XLA Ops:
  0.0 2.7 %pack.1 = (bf16[128,640]{1,0:T(8,128)(2,1)S(1)}, bf16[256,640]{1,0:T(8,128)(2,1)S(1)}, bf16[256,640]{1,0:T(8,128)(2,1)S(1)}, bf16[256,640]{1,0:T(8,128)(2,1)S(1)...) custom-call(s32[4,8]{1,0:T(4,128)} %ids.1, bf16[16,64,1280]{2,1,0:T(8,128)(2,1)} %keys.1, ...), custom_call_target="tpu_custom_call" | custom-call | bytes 12582912 | tf_op jit(solution)/shard_map/pack/pallas_call | solution.py:118
  2.7 0.5 collective-permute-start
  3.2 2.6 %collective-permute-start.5 = (bf16[1280,640]{1,0:T(8,128)(2,1)S(1)}, bf16[1280,640]{1,0:T(8,128)(2,1)S(1)}, u32[]{:S(2)}, u32[]{:S(2)}) collective-permute-start(bf16[1280,640]{1,0:T(8,128)(2,1)S(1)} %get-tuple-element.28), channel_id=1, source_target_pairs={{0,2},{2,0},{1,3},{3,1},{4,6},{6,4},{5,7},{7,5},{8,10},{10,8},{9,1... | collective-permute-start | bytes 4915208 | tf_op jit(solution)/shard_map/ppermute | solution.py:473
  5.8 3.6 %collective-permute-start.1 = (bf16[256,640]{1,0:T(8,128)(2,1)S(1)}, bf16[256,640]{1,0:T(8,128)(2,1)S(1)}, u32[]{:S(2)}, u32[]{:S(2)}) collective-permute-start(bf16[256,640]{1,0:T(8,128)(2,1)S(1)} %get-tuple-element.24), channel_id=1, source_target_pairs={{0,12},{4,8},{8,4},{12,0},{1,13},{5,9},{9,5},{13,1},{2,14},{6,10},... | collective-permute-start | bytes 983048 | tf_op jit(solution)/shard_map/ppermute | solution.py:472
  9.4 0.8 collective-permute-start.3
  10.2 11.3 %attend_current.1 = (f32[5,1024,128]{2,1,0:T(8,128)S(1)}, f32[5,1024,128]{2,1,0:T(8,128)S(1)}, bf16[1024,640]{1,0:T(8,128)(2,1)S(1)}) custom-call(bf16[1024,1280]{1,0:T(8,128)(2,1)} %queries.1, bf16[512,1280]{1,0:T(8,128)(2,1)} %own_keys.1, bf16[512,1280]{1,0:T(8,128)(2,1)} %own_values.1, bf16[1152,640]{1,0:T(8,128)(2,1)S(1)} %collective-permute-done.sibling.rest_0_.rest_4_), custom_call_target="tpu_custom_call" | custom-call | flops 4026531840 | bytes 7864320 | tf_op jit(solution)/shard_map/attend_current/pallas_call | solution.py:255
  21.5 3.6 %load.1 = (bf16[1280,2560]{1,0:T(8,128)(2,1)S(1)}, f32[8,64]{1,0:T(8,128)S(1)}) custom-call(s32[4,8]{1,0:T(4,128)} %ids.1, s32[128]{0:T(128)} %counts.1, bf16[1280,2560]{1,0:T(8,128)(2,1)} %weight.3, f32[5,1024,128]{2,1,0:T(8,128)S(1)} %get-tuple-element.19.after.lse), custom_call_target="tpu_custom_call" | custom-call | bytes 6553600 | tf_op jit(solution)/shard_map/load/pallas_call | solution.py:174
  25.1 12.5 %collective-permute-done.2.refs_1_.rest_2_ = bf16[256,640]{1,0:T(8,128)(2,1)S(1)} collective-permute-done((bf16[256,640]{1,0:T(8,128)(2,1)S(1)}, bf16[256,640]{1,0:T(8,128)(2,1)S(1)}, u32[]{:S(2)}, u32[]{:S(2)}) %collective-permute-start.2) | collective-permute-done | bytes 327712 | tf_op jit(solution)/shard_map/ppermute | solution.py:472
  37.8 1.4 %far_first.1 = (f32[5,512,128]{2,1,0:T(8,128)S(1)}, f32[5,512,128]{2,1,0:T(8,128)S(1)}) custom-call(f32[8,64]{1,0:T(8,128)S(1)} %get-tuple-element.20.bias, bf16[1024,640]{1,0:T(8,128)(2,1)S(1)} %get-tuple-element.21.q, f32[5,1024,128]{2,1,0:T(8,128)S(1)} %get-tuple-element.22.held, f32[5,1024,128]{2,1,0:T(8,128)S(1)} %get-tuple-element.19.after.lse, ...), custom_call_target="tpu_custom_call" | custom-call | flops 1024 | bytes 1024 | tf_op jit(solution)/shard_map/far_first/pallas_call | solution.py:328
  39.6 1.4 %far_last.1.after.mine = bf16[512,640]{1,0:T(8,128)(2,1)S(1)} custom-call(f32[8,64]{1,0:T(8,128)S(1)} %get-tuple-element.20.bias, bf16[1024,640]{1,0:T(8,128)(2,1)S(1)} %get-tuple-element.21.q, f32[5,512,128]{2,1,0:T(8,128)S(1)} %get-tuple-element.29.held, f32[5,512,128]{2,1,0:T(8,128)S(1)} %get-tuple-element.30.lse, ...), custom_call_target="tpu_custom_call" | custom-call | flops 1024 | bytes 1024 | tf_op jit(solution)/shard_map/far_last/pallas_call | solution.py:328
  41.2 0.6 collective-permute-start.7
  42.3 1.9 %collective-permute-start.12 = (bf16[1280,512]{1,0:T(8,128)(2,1)S(1)}, bf16[1280,512]{1,0:T(8,128)(2,1)S(1)}, u32[]{:S(2)}, u32[]{:S(2)}) collective-permute-start(bf16[1280,512]{1,0:T(8,128)(2,1)S(1)} %leading.1.rest_8_), channel_id=1, source_target_pairs={{0,16},{16,0},{1,17},{17,1},{2,18},{18,2},{3,19},{19,3},{4,20},{20... | collective-permute-start | bytes 3932168 | tf_op jit(solution)/shard_map/ppermute | solution.py:488
  44.1 1.7 %collective-permute-start.11 = (bf16[1280,512]{1,0:T(8,128)(2,1)S(1)}, bf16[1280,512]{1,0:T(8,128)(2,1)S(1)}, u32[]{:S(2)}, u32[]{:S(2)}) collective-permute-start(bf16[1280,512]{1,0:T(8,128)(2,1)S(1)} %leading.1.rest_8_), channel_id=1, source_target_pairs={{0,4},{4,0},{8,12},{12,8},{1,5},{5,1},{9,13},{13,9},{2,6},{6,2},{1... | collective-permute-start | bytes 3932168 | tf_op jit(solution)/shard_map/ppermute | solution.py:489
  45.8 2.1 %near.1.rest_0_.mine = bf16[512,640]{1,0:T(8,128)(2,1)S(1)} custom-call(f32[8,64]{1,0:T(8,128)S(1)} %get-tuple-element.20.bias, bf16[1024,640]{1,0:T(8,128)(2,1)S(1)} %get-tuple-element.21.q, f32[5,1024,128]{2,1,0:T(8,128)S(1)} %get-tuple-element.22.held, f32[5,1024,128]{2,1,0:T(8,128)S(1)} %get-tuple-element.19.after.lse, ...), custom_call_target="tpu_custom_call" | custom-call | flops 1024 | bytes 1024 | tf_op jit(solution)/shard_map/near/pallas_call | solution.py:328
  47.9 1.9 %project_unshared.1.refs_1_ = bf16[512,896]{1,0:T(8,128)(2,1)S(1)} custom-call(bf16[512,640]{1,0:T(8,128)(2,1)S(1)} %far_last.1.after.mine, bf16[512,640]{1,0:T(8,128)(2,1)S(1)} %collective-permute-done.8.other, bf16[1280,2560]{1,0:T(8,128)(2,1)S(1)} %get-tuple-element.27.refs_3_.weight, bf16[512,640]{1,0:T(8,128)(2,1)S(1)} %near.1.rest_0_.mine), custom_call_target="tpu_custom_call" | custom-call | flops 1024 | bytes 1024 | tf_op jit(solution)/shard_map/project_unshared/pallas_call | solution.py:378
  49.8 1.9 %collective-permute-start.9 = (bf16[512,896]{1,0:T(8,128)(2,1)S(1)}, bf16[512,896]{1,0:T(8,128)(2,1)S(1)}, u32[]{:S(2)}, u32[]{:S(2)}) collective-permute-start(bf16[512,896]{1,0:T(8,128)(2,1)S(1)} %project_unshared.1.refs_1_), channel_id=1, source_target_pairs={{0,2},{2,0},{1,3},{3,1},{4,6},{6,4},{5,7},{7,5},{8,10},{10,8},{9,1... | collective-permute-start | bytes 2752520 | tf_op jit(solution)/shard_map/ppermute | solution.py:495
  51.7 7.1 %collective-permute-done.7.refs_0_ = bf16[512,640]{1,0:T(8,128)(2,1)S(1)} collective-permute-done((bf16[512,640]{1,0:T(8,128)(2,1)S(1)}, bf16[512,640]{1,0:T(8,128)(2,1)S(1)}, u32[]{:S(2)}, u32[]{:S(2)}) %collective-permute-start.7) | collective-permute-done | bytes 655392 | tf_op jit(solution)/shard_map/ppermute | solution.py:485
  58.8 4.4 %project.1.refs_0_.terms = bf16[512,2560]{1,0:T(8,128)(2,1)S(1)} custom-call(bf16[512,640]{1,0:T(8,128)(2,1)S(1)} %near.1.rest_0_.mine, bf16[512,640]{1,0:T(8,128)(2,1)S(1)} %collective-permute-done.6.other, bf16[1280,2560]{1,0:T(8,128)(2,1)S(1)} %get-tuple-element.27.refs_3_.weight, bf16[512,640]{1,0:T(8,128)(2,1)S(1)} %gate.1.rest_0_.refs_1_.mine), custom_call_target="tpu_custom_call" | custom-call | flops 1024 | bytes 1024 | tf_op jit(solution)/shard_map/project/pallas_call | solution.py:378
  63.2 2.1 %add_remote.3.total = bf16[512,2560]{1,0:T(8,128)(2,1)} custom-call(bf16[512,2560]{1,0:T(8,128)(2,1)S(1)} %project.1.refs_0_.terms, bf16[512,640]{1,0:T(8,128)(2,1)S(1)} %gate.1.rest_0_.refs_1_.mine, bf16[512,640]{1,0:T(8,128)(2,1)S(1)} %collective-permute-done.10.refs_2_.other, bf16[1280,640]{1,0:T(8,128)(2,1)S(1)} %collective-permute-done.5.array.refs_3_), custom_call_target="tpu_custom_call" | custom-call | flops 1024 | bytes 1024 | tf_op jit(solution)/shard_map/add_remote/pallas_call | solution.py:435
  65.3 7.6 %collective-permute-done.12.weight = bf16[1280,512]{1,0:T(8,128)(2,1)S(1)} collective-permute-done((bf16[1280,512]{1,0:T(8,128)(2,1)S(1)}, bf16[1280,512]{1,0:T(8,128)(2,1)S(1)}, u32[]{:S(2)}, u32[]{:S(2)}) %collective-permute-start.12) | collective-permute-done | bytes 1310752 | tf_op jit(solution)/shard_map/ppermute | solution.py:488
  72.9 1.7 %add_remote.4.total = bf16[512,2560]{1,0:T(8,128)(2,1)} custom-call(bf16[512,2560]{1,0:T(8,128)(2,1)S(1)} %project.1.refs_0_.terms, bf16[512,640]{1,0:T(8,128)(2,1)S(1)} %gate.1.rest_0_.refs_1_.mine, bf16[512,640]{1,0:T(8,128)(2,1)S(1)} %collective-permute-done.10.refs_2_.other, ...), custom_call_target="tpu_custom_call", output_to_operand_aliasing={{}: (4, {})} | custom-call | flops 1024 | bytes 1024 | tf_op jit(solution)/shard_map/add_remote/pallas_call | solution.py:435
  74.6 1.7 %add_remote.5.total = bf16[512,2560]{1,0:T(8,128)(2,1)} custom-call(bf16[512,2560]{1,0:T(8,128)(2,1)S(1)} %project.1.refs_0_.terms, bf16[512,640]{1,0:T(8,128)(2,1)S(1)} %gate.1.rest_0_.refs_1_.mine, bf16[512,640]{1,0:T(8,128)(2,1)S(1)} %collective-permute-done.10.refs_2_.other, ...), custom_call_target="tpu_custom_call", output_to_operand_aliasing={{}: (4, {})} | custom-call | flops 1024 | bytes 1024 | tf_op jit(solution)/shard_map/add_remote/pallas_call | solution.py:435
  76.3 1.6 %collective-permute-done.9.came = bf16[512,896]{1,0:T(8,128)(2,1)S(1)} collective-permute-done((bf16[512,896]{1,0:T(8,128)(2,1)S(1)}, bf16[512,896]{1,0:T(8,128)(2,1)S(1)}, u32[]{:S(2)}, u32[]{:S(2)}) %collective-permute-start.9) | collective-permute-done | bytes 917536 | tf_op jit(solution)/shard_map/ppermute | solution.py:495
  77.9 1.1 %add_unshared.1 = bf16[512,2560]{1,0:T(8,128)(2,1)} custom-call(bf16[512,2560]{1,0:T(8,128)(2,1)S(1)} %project.1.refs_0_.terms, bf16[512,896]{1,0:T(8,128)(2,1)S(1)} %collective-permute-done.9.came, bf16[512,2560]{1,0:T(8,128)(2,1)} %add_remote.5.total), custom_call_target="tpu_custom_call", output_to_operand_aliasing={{}: (2, {})} | custom-call | flops 1024 | bytes 1024 | tf_op jit(solution)/shard_map/add_unshared/pallas_call | solution.py:435
  (17 shorter events, 1.3 us)
Async XLA Ops:
  2.7 7.5 %collective-permute-start = (bf16[1152,640]{1,0:T(8,128)(2,1)S(1)}, bf16[1152,640]{1,0:T(8,128)(2,1)S(1)}, u32[]{:S(2)}, u32[]{:S(2)}) collective-permute-start(bf16[1152,640]{1,0:T(8,128)(2,1)S(1)} %get-tuple-element.18), channel_id=1, source_target_pairs={{0,1},{1,0},{2,3},{3,2},{4,5},{5,4},{6,7},{7,6},{8,9},{9,8},{10,11... | collective-permute-start | bytes 4423688 | tf_op jit(solution)/shard_map/ppermute | solution.py:474
  3.2 39.0 %collective-permute-start.5 = (bf16[1280,640]{1,0:T(8,128)(2,1)S(1)}, bf16[1280,640]{1,0:T(8,128)(2,1)S(1)}, u32[]{:S(2)}, u32[]{:S(2)}) collective-permute-start(bf16[1280,640]{1,0:T(8,128)(2,1)S(1)} %get-tuple-element.28), channel_id=1, source_target_pairs={{0,2},{2,0},{1,3},{3,1},{4,6},{6,4},{5,7},{7,5},{8,10},{10,8},{9,1... | collective-permute-start | bytes 4915208 | tf_op jit(solution)/shard_map/ppermute | solution.py:473
  5.8 19.3 %collective-permute-start.1 = (bf16[256,640]{1,0:T(8,128)(2,1)S(1)}, bf16[256,640]{1,0:T(8,128)(2,1)S(1)}, u32[]{:S(2)}, u32[]{:S(2)}) collective-permute-start(bf16[256,640]{1,0:T(8,128)(2,1)S(1)} %get-tuple-element.24), channel_id=1, source_target_pairs={{0,12},{4,8},{8,4},{12,0},{1,13},{5,9},{9,5},{13,1},{2,14},{6,10},... | collective-permute-start | bytes 983048 | tf_op jit(solution)/shard_map/ppermute | solution.py:472
  9.4 28.3 %collective-permute-start.2 = (bf16[256,640]{1,0:T(8,128)(2,1)S(1)}, bf16[256,640]{1,0:T(8,128)(2,1)S(1)}, u32[]{:S(2)}, u32[]{:S(2)}) collective-permute-start(bf16[256,640]{1,0:T(8,128)(2,1)S(1)} %get-tuple-element.25), channel_id=1, source_target_pairs={{0,8},{4,12},{8,0},{12,4},{1,9},{5,13},{9,1},{13,5},{2,10},{6,14},... | collective-permute-start | bytes 983048 | tf_op jit(solution)/shard_map/ppermute | solution.py:472
  9.4 28.3 %collective-permute-start.3 = (bf16[256,640]{1,0:T(8,128)(2,1)S(1)}, bf16[256,640]{1,0:T(8,128)(2,1)S(1)}, u32[]{:S(2)}, u32[]{:S(2)}) collective-permute-start(bf16[256,640]{1,0:T(8,128)(2,1)S(1)} %get-tuple-element.26), channel_id=1, source_target_pairs={{0,4},{4,0},{8,12},{12,8},{1,5},{5,1},{9,13},{13,9},{2,6},{6,2},{1... | collective-permute-start | bytes 983048 | tf_op jit(solution)/shard_map/ppermute | solution.py:472
  37.7 1.9 %collective-permute-start.4 = (bf16[384,640]{1,0:T(8,128)(2,1)S(1)}, bf16[384,640]{1,0:T(8,128)(2,1)S(1)}, u32[]{:S(2)}, u32[]{:S(2)}) collective-permute-start(bf16[384,640]{1,0:T(8,128)(2,1)S(1)} %pass_on.1.rest_4_), channel_id=1, source_target_pairs={{0,1},{1,0},{2,3},{3,2},{4,5},{5,4},{6,7},{7,6},{8,9},{9,8},{10,11... | collective-permute-start | bytes 1474568 | tf_op jit(solution)/shard_map/ppermute | solution.py:479
  41.0 6.9 %collective-permute-start.8 = (bf16[512,640]{1,0:T(8,128)(2,1)S(1)}, bf16[512,640]{1,0:T(8,128)(2,1)S(1)}, u32[]{:S(2)}, u32[]{:S(2)}) collective-permute-start(bf16[512,640]{1,0:T(8,128)(2,1)S(1)} %far_last.1.after.mine), channel_id=1, source_target_pairs={{0,1},{1,0},{2,3},{3,2},{4,5},{5,4},{6,7},{7,6},{8,9},{9,8},{10,11... | collective-permute-start | bytes 1966088 | tf_op jit(solution)/shard_map/ppermute | solution.py:486
  41.2 17.6 %collective-permute-start.7 = (bf16[512,640]{1,0:T(8,128)(2,1)S(1)}, bf16[512,640]{1,0:T(8,128)(2,1)S(1)}, u32[]{:S(2)}, u32[]{:S(2)}) collective-permute-start(bf16[512,640]{1,0:T(8,128)(2,1)S(1)} %far_last.1.after.mine), channel_id=1, source_target_pairs={{0,2},{2,0},{1,3},{3,1},{4,6},{6,4},{5,7},{7,5},{8,10},{10,8},{9,1... | collective-permute-start | bytes 1966088 | tf_op jit(solution)/shard_map/ppermute | solution.py:485
  42.3 30.6 %collective-permute-start.12 = (bf16[1280,512]{1,0:T(8,128)(2,1)S(1)}, bf16[1280,512]{1,0:T(8,128)(2,1)S(1)}, u32[]{:S(2)}, u32[]{:S(2)}) collective-permute-start(bf16[1280,512]{1,0:T(8,128)(2,1)S(1)} %leading.1.rest_8_), channel_id=1, source_target_pairs={{0,16},{16,0},{1,17},{17,1},{2,18},{18,2},{3,19},{19,3},{4,20},{20... | collective-permute-start | bytes 3932168 | tf_op jit(solution)/shard_map/ppermute | solution.py:488
  44.1 30.5 %collective-permute-start.11 = (bf16[1280,512]{1,0:T(8,128)(2,1)S(1)}, bf16[1280,512]{1,0:T(8,128)(2,1)S(1)}, u32[]{:S(2)}, u32[]{:S(2)}) collective-permute-start(bf16[1280,512]{1,0:T(8,128)(2,1)S(1)} %leading.1.rest_8_), channel_id=1, source_target_pairs={{0,4},{4,0},{8,12},{12,8},{1,5},{5,1},{9,13},{13,9},{2,6},{6,2},{1... | collective-permute-start | bytes 3932168 | tf_op jit(solution)/shard_map/ppermute | solution.py:489
  49.8 28.1 %collective-permute-start.9 = (bf16[512,896]{1,0:T(8,128)(2,1)S(1)}, bf16[512,896]{1,0:T(8,128)(2,1)S(1)}, u32[]{:S(2)}, u32[]{:S(2)}) collective-permute-start(bf16[512,896]{1,0:T(8,128)(2,1)S(1)} %project_unshared.1.refs_1_), channel_id=1, source_target_pairs={{0,2},{2,0},{1,3},{3,1},{4,6},{6,4},{5,7},{7,5},{8,10},{10,8},{9,1... | collective-permute-start | bytes 2752520 | tf_op jit(solution)/shard_map/ppermute | solution.py:495
  51.7 7.1 %collective-permute-start.6 = (bf16[512,640]{1,0:T(8,128)(2,1)S(1)}, bf16[512,640]{1,0:T(8,128)(2,1)S(1)}, u32[]{:S(2)}, u32[]{:S(2)}) collective-permute-start(bf16[512,640]{1,0:T(8,128)(2,1)S(1)} %near.1.rest_0_.mine), channel_id=1, source_target_pairs={{0,1},{1,0},{2,3},{3,2},{4,5},{5,4},{6,7},{7,6},{8,9},{9,8},{10,11... | collective-permute-start | bytes 1966088 | tf_op jit(solution)/shard_map/ppermute | solution.py:492
  58.8 4.4 %collective-permute-start.10 = (bf16[512,640]{1,0:T(8,128)(2,1)S(1)}, bf16[512,640]{1,0:T(8,128)(2,1)S(1)}, u32[]{:S(2)}, u32[]{:S(2)}) collective-permute-start(bf16[512,640]{1,0:T(8,128)(2,1)S(1)} %gate.1.rest_0_.refs_1_.mine), channel_id=1, source_target_pairs={{0,1},{1,0},{2,3},{3,2},{4,5},{5,4},{6,7},{7,6},{8,9},{9,8},{10,11... | collective-permute-start | bytes 1966088 | tf_op jit(solution)/shard_map/ppermute | solution.py:497

commit v3 on v2

--- a/solution.py
+++ b/solution.py
@@ -49,8 +49,14 @@
         copy.wait()
 
 
-def exchange_order(seq_count):
-    return [0, *range(seq_count - 1, 0, -1)]
+def exchange_orders(seq_count):
+    across, beside = list(range(seq_count // 2, seq_count)), list(range(1, seq_count // 2))
+    return [0, *across, *beside], [0, *reversed(across), *beside]
+
+
+def exchange_flip(place, sub, seq_count):
+    first, second = exchange_orders(seq_count)
+    return jnp.where(sub == 0, jnp.int32(first[place]), jnp.int32(second[place]))
 
 
 def held_by(ids, stretch, owner, count):
@@ -94,14 +100,15 @@
         span = pl.ds(part * rows, rows)
         start(weight.at[span, pl.ds(first, block)], columns_out.at[span, :])
     listed.wait()
-    for flip, out in zip(exchange_order(seq_count), outs):
+    for place, out in enumerate(outs):
+        flip = exchange_flip(place, sub_index, seq_count)
         owner = seq_index * 2 + sub_index
         wanted = held_by(ids, lax.bitwise_xor(seq_index, flip), owner, frame_count) - owner * FR_DEV
         wanted = jnp.clip(wanted, 0, FR_DEV - 1)
         for turn in range(2):
             half = sub_index if turn == 0 else 1 - sub_index
             for part, source in enumerate((keys, values)):
-                if flip == 0 and turn == 1:
+                if place == 0 and turn == 1:
                     target = sibling.at[pl.ds(2 * count + part * FT, FT), :]
                 else:
                     target = out.at[pl.ds((2 * turn + part) * FT, FT), :]
@@ -161,8 +168,8 @@
     slot = lax.broadcasted_iota(jnp.int32, (1, FT), 1)
     for index in range(2 * seq_count):
         turn, place = divmod(index, seq_count)
-        source = lax.bitwise_xor(seq_index, exchange_order(seq_count)[place]) * 2
-        owner = source + (sub_index if turn == 0 else 1 - sub_index)
+        source_sub = sub_index if turn == 0 else 1 - sub_index
+        owner = lax.bitwise_xor(seq_index, exchange_flip(place, source_sub, seq_count)) * 2 + source_sub
         live = slot < counts[held_by(ids, seq_index, owner, 2 * seq_count)]
         mask[pl.ds(index, 1), :] = jnp.where(live, 0.0, MASKED).astype(F32)
     for copy in copies:
@@ -468,8 +475,10 @@
         frame_ids, mem_keys, mem_values, cur_keys, cur_values, out_weight, low, share, seq_count
     )
     mine = [sends[0]]
-    for flip, sent in list(zip(exchange_order(seq_count), sends))[1:]:
-        mine.append(lax.ppermute(sent, "seq", [(index, index ^ flip) for index in range(seq_count)]))
+    for place in range(1, seq_count):
+        flips = [order[place] for order in exchange_orders(seq_count)]
+        pairs = [(2 * seq + sub, 2 * (seq ^ flip) + sub) for seq in range(seq_count) for sub, flip in enumerate(flips)]
+        mine.append(lax.ppermute(sends[place], ("seq", "sub"), pairs))
     columns = lax.ppermute(columns, "head", SWAP)
     sibling = lax.ppermute(to_sibling, "sub", SWAP)
 

time: 79.3 us -> 78 us (0.984)
  waiting for transfers between devices: 29.6 us -> 22.8 us
  starting transfers between devices: 13.7 us -> 19.4 us
    ppermute x3, waiting for transfers between devices: 12.5 us -> 6.37 us  [local(): mine.append(lax.ppermute(sends[place], ('seq', 'sub'), pairs))]
    ppermute x1, starting transfers between devices: 0.07 us -> 5.61 us  [local(): theirs = lax.ppermute(passed, 'sub', SWAP)]
    ppermute x1, waiting for transfers between devices: 1.62 us -> 0.41 us  [local(): came = lax.ppermute(term, 'head', SWAP)]
    ppermute x1, waiting for transfers between devices: 7.58 us -> 8.53 us  [local(): group_columns = lax.ppermute(columns_copy, 'groups', SWAP)]
  transfers between devices with their start and end apart: 13 -> 13, of which waited for: 6 -> 6; matrix products, arithmetic and copies ran while one was open for 0% -> 0% of each run, Pallas kernels for 40% -> 41%
where the time goes in v3:
time: 78 us; the launch traced here: 77.8 us
  Pallas kernels  35.5 us (46%)
  waiting for transfers between devices  22.8 us (29%)
  starting transfers between devices  19.4 us (25%)
    pallas_call x1, Pallas kernels, attend_current(): pl.pallas_call(functools.partial(current_kernel, 512), in_specs=[HBM] * 3...  11.3 us
    ppermute x1, waiting for transfers between devices, local(): group_columns = lax.ppermute(columns_copy, 'groups', SWAP)  8.53 us
    pallas_call x4, Pallas kernels, finish_block(): pl.pallas_call(body, in_specs=[VMEM] * count + [HBM] * len(totals), out_s...  6.6 us
    ppermute x1, waiting for transfers between devices, local(): came_mine = lax.ppermute(far, 'head', SWAP)  6.41 us
    ppermute x3, waiting for transfers between devices, local(): mine.append(lax.ppermute(sends[place], ('seq', 'sub'), pairs))  6.37 us
    pallas_call x2, Pallas kernels, project_call(): pl.pallas_call(kernel, in_specs=[VMEM] * 3 + [ANY] * len(after), out_spec...  6.28 us
    ppermute x1, starting transfers between devices, local(): theirs = lax.ppermute(passed, 'sub', SWAP)  5.61 us
    pallas_call x3, Pallas kernels, attend_frames(): pl.pallas_call(functools.partial(frames_kernel, heads, half, state_half,...  4.88 us
  transfers between devices with their start and end apart: 13, of which 6 were waited for; matrix products, arithmetic and copies ran while one was open for 0% of the time, Pallas kernels for 41%

profile of v3, /device:TPU:0, one launch (start us, length us, event | category | flops | bytes accessed | tf_op | source)
XLA Modules:
  0.0 77.8 jit_solution(3626488903897556639)
XLA Ops:
  0.0 2.7 %pack.1 = (bf16[128,640]{1,0:T(8,128)(2,1)S(1)}, bf16[256,640]{1,0:T(8,128)(2,1)S(1)}, bf16[256,640]{1,0:T(8,128)(2,1)S(1)}, bf16[256,640]{1,0:T(8,128)(2,1)S(1)...) custom-call(s32[4,8]{1,0:T(4,128)} %ids.1, bf16[16,64,1280]{2,1,0:T(8,128)(2,1)} %keys.1, ...), custom_call_target="tpu_custom_call" | custom-call | bytes 12582912 | tf_op jit(solution)/shard_map/pack/pallas_call | solution.py:125
  3.2 2.6 %collective-permute-start.5 = (bf16[1280,640]{1,0:T(8,128)(2,1)S(1)}, bf16[1280,640]{1,0:T(8,128)(2,1)S(1)}, u32[]{:S(2)}, u32[]{:S(2)}) collective-permute-start(bf16[1280,640]{1,0:T(8,128)(2,1)S(1)} %get-tuple-element.28), channel_id=1, source_target_pairs={{0,2},{2,0},{1,3},{3,1},{4,6},{6,4},{5,7},{7,5},{8,10},{10,8},{9,1... | collective-permute-start | bytes 4915208 | tf_op jit(solution)/shard_map/ppermute | solution.py:482
  5.8 2.6 %collective-permute-start.1 = (bf16[256,640]{1,0:T(8,128)(2,1)S(1)}, bf16[256,640]{1,0:T(8,128)(2,1)S(1)}, u32[]{:S(2)}, u32[]{:S(2)}) collective-permute-start(bf16[256,640]{1,0:T(8,128)(2,1)S(1)} %get-tuple-element.24), channel_id=1, source_target_pairs={{0,8},{1,13},{4,12},{5,9},{8,0},{9,5},{12,4},{13,1},{2,10},{3,15},... | collective-permute-start | bytes 983048 | tf_op jit(solution)/shard_map/ppermute | solution.py:481
  8.4 1.3 %collective-permute-start.2 = (bf16[256,640]{1,0:T(8,128)(2,1)S(1)}, bf16[256,640]{1,0:T(8,128)(2,1)S(1)}, u32[]{:S(2)}, u32[]{:S(2)}) collective-permute-start(bf16[256,640]{1,0:T(8,128)(2,1)S(1)} %get-tuple-element.25), channel_id=1, source_target_pairs={{0,12},{1,9},{4,8},{5,13},{8,4},{9,1},{12,0},{13,5},{2,14},{3,11},... | collective-permute-start | bytes 983048 | tf_op jit(solution)/shard_map/ppermute | solution.py:481
  10.0 11.3 %attend_current.1 = (f32[5,1024,128]{2,1,0:T(8,128)S(1)}, f32[5,1024,128]{2,1,0:T(8,128)S(1)}, bf16[1024,640]{1,0:T(8,128)(2,1)S(1)}) custom-call(bf16[1024,1280]{1,0:T(8,128)(2,1)} %queries.1, bf16[512,1280]{1,0:T(8,128)(2,1)} %own_keys.1, bf16[512,1280]{1,0:T(8,128)(2,1)} %own_values.1, bf16[1152,640]{1,0:T(8,128)(2,1)S(1)} %collective-permute-done.sibling.rest_0_.rest_4_), custom_call_target="tpu_custom_call" | custom-call | flops 4026531840 | bytes 7864320 | tf_op jit(solution)/shard_map/attend_current/pallas_call | solution.py:262
  21.3 3.6 %load.1 = (bf16[1280,2560]{1,0:T(8,128)(2,1)S(1)}, f32[8,64]{1,0:T(8,128)S(1)}) custom-call(s32[4,8]{1,0:T(4,128)} %ids.1, s32[128]{0:T(128)} %counts.1, bf16[1280,2560]{1,0:T(8,128)(2,1)} %weight.3, f32[5,1024,128]{2,1,0:T(8,128)S(1)} %get-tuple-element.19.after.lse), custom_call_target="tpu_custom_call" | custom-call | bytes 6553600 | tf_op jit(solution)/shard_map/load/pallas_call | solution.py:181
  24.9 6.4 %collective-permute-done.1.refs_0_.rest_1_ = bf16[256,640]{1,0:T(8,128)(2,1)S(1)} collective-permute-done((bf16[256,640]{1,0:T(8,128)(2,1)S(1)}, bf16[256,640]{1,0:T(8,128)(2,1)S(1)}, u32[]{:S(2)}, u32[]{:S(2)}) %collective-permute-start.1) | collective-permute-done | bytes 327712 | tf_op jit(solution)/shard_map/ppermute | solution.py:481
  31.3 5.6 %collective-permute-start.4 = (bf16[384,640]{1,0:T(8,128)(2,1)S(1)}, bf16[384,640]{1,0:T(8,128)(2,1)S(1)}, u32[]{:S(2)}, u32[]{:S(2)}) collective-permute-start(bf16[384,640]{1,0:T(8,128)(2,1)S(1)} %pass_on.1.rest_4_), channel_id=1, source_target_pairs={{0,1},{1,0},{2,3},{3,2},{4,5},{5,4},{6,7},{7,6},{8,9},{9,8},{10,11... | collective-permute-start | bytes 1474568 | tf_op jit(solution)/shard_map/ppermute | solution.py:488
  36.9 1.4 %far_first.1 = (f32[5,512,128]{2,1,0:T(8,128)S(1)}, f32[5,512,128]{2,1,0:T(8,128)S(1)}) custom-call(f32[8,64]{1,0:T(8,128)S(1)} %get-tuple-element.20.bias, bf16[1024,640]{1,0:T(8,128)(2,1)S(1)} %get-tuple-element.21.q, f32[5,1024,128]{2,1,0:T(8,128)S(1)} %get-tuple-element.22.held, f32[5,1024,128]{2,1,0:T(8,128)S(1)} %get-tuple-element.19.after.lse, ...), custom_call_target="tpu_custom_call" | custom-call | flops 1024 | bytes 1024 | tf_op jit(solution)/shard_map/far_first/pallas_call | solution.py:335
  38.4 1.4 %far_last.1.after.mine = bf16[512,640]{1,0:T(8,128)(2,1)S(1)} custom-call(f32[8,64]{1,0:T(8,128)S(1)} %get-tuple-element.20.bias, bf16[1024,640]{1,0:T(8,128)(2,1)S(1)} %get-tuple-element.21.q, f32[5,512,128]{2,1,0:T(8,128)S(1)} %get-tuple-element.29.held, f32[5,512,128]{2,1,0:T(8,128)S(1)} %get-tuple-element.30.lse, ...), custom_call_target="tpu_custom_call" | custom-call | flops 1024 | bytes 1024 | tf_op jit(solution)/shard_map/far_last/pallas_call | solution.py:335
  40.3 0.9 %collective-permute-start.7 = (bf16[512,640]{1,0:T(8,128)(2,1)S(1)}, bf16[512,640]{1,0:T(8,128)(2,1)S(1)}, u32[]{:S(2)}, u32[]{:S(2)}) collective-permute-start(bf16[512,640]{1,0:T(8,128)(2,1)S(1)} %far_last.1.after.mine), channel_id=1, source_target_pairs={{0,2},{2,0},{1,3},{3,1},{4,6},{6,4},{5,7},{7,5},{8,10},{10,8},{9,1... | collective-permute-start | bytes 1966088 | tf_op jit(solution)/shard_map/ppermute | solution.py:494
  41.2 1.0 %collective-permute-done.5.array.refs_3_ = bf16[1280,640]{1,0:T(8,128)(2,1)S(1)} collective-permute-done((bf16[1280,640]{1,0:T(8,128)(2,1)S(1)}, bf16[1280,640]{1,0:T(8,128)(2,1)S(1)}, u32[]{:S(2)}, u32[]{:S(2)}) %collective-permute-start.5) | collective-permute-done | bytes 1638432 | tf_op jit(solution)/shard_map/ppermute | solution.py:482
  42.3 1.9 %collective-permute-start.12 = (bf16[1280,512]{1,0:T(8,128)(2,1)S(1)}, bf16[1280,512]{1,0:T(8,128)(2,1)S(1)}, u32[]{:S(2)}, u32[]{:S(2)}) collective-permute-start(bf16[1280,512]{1,0:T(8,128)(2,1)S(1)} %leading.1.rest_8_), channel_id=1, source_target_pairs={{0,16},{16,0},{1,17},{17,1},{2,18},{18,2},{3,19},{19,3},{4,20},{20... | collective-permute-start | bytes 3932168 | tf_op jit(solution)/shard_map/ppermute | solution.py:497
  44.1 1.6 %collective-permute-start.11 = (bf16[1280,512]{1,0:T(8,128)(2,1)S(1)}, bf16[1280,512]{1,0:T(8,128)(2,1)S(1)}, u32[]{:S(2)}, u32[]{:S(2)}) collective-permute-start(bf16[1280,512]{1,0:T(8,128)(2,1)S(1)} %leading.1.rest_8_), channel_id=1, source_target_pairs={{0,4},{4,0},{8,12},{12,8},{1,5},{5,1},{9,13},{13,9},{2,6},{6,2},{1... | collective-permute-start | bytes 3932168 | tf_op jit(solution)/shard_map/ppermute | solution.py:498
  45.7 2.1 %near.1.rest_0_.mine = bf16[512,640]{1,0:T(8,128)(2,1)S(1)} custom-call(f32[8,64]{1,0:T(8,128)S(1)} %get-tuple-element.20.bias, bf16[1024,640]{1,0:T(8,128)(2,1)S(1)} %get-tuple-element.21.q, f32[5,1024,128]{2,1,0:T(8,128)S(1)} %get-tuple-element.22.held, f32[5,1024,128]{2,1,0:T(8,128)S(1)} %get-tuple-element.19.after.lse, ...), custom_call_target="tpu_custom_call" | custom-call | flops 1024 | bytes 1024 | tf_op jit(solution)/shard_map/near/pallas_call | solution.py:335
  47.8 1.9 %project_unshared.1.refs_1_ = bf16[512,896]{1,0:T(8,128)(2,1)S(1)} custom-call(bf16[512,640]{1,0:T(8,128)(2,1)S(1)} %far_last.1.after.mine, bf16[512,640]{1,0:T(8,128)(2,1)S(1)} %collective-permute-done.8.other, bf16[1280,2560]{1,0:T(8,128)(2,1)S(1)} %get-tuple-element.27.refs_3_.weight, bf16[512,640]{1,0:T(8,128)(2,1)S(1)} %near.1.rest_0_.mine), custom_call_target="tpu_custom_call" | custom-call | flops 1024 | bytes 1024 | tf_op jit(solution)/shard_map/project_unshared/pallas_call | solution.py:385
  49.7 1.7 %collective-permute-start.9 = (bf16[512,896]{1,0:T(8,128)(2,1)S(1)}, bf16[512,896]{1,0:T(8,128)(2,1)S(1)}, u32[]{:S(2)}, u32[]{:S(2)}) collective-permute-start(bf16[512,896]{1,0:T(8,128)(2,1)S(1)} %project_unshared.1.refs_1_), channel_id=1, source_target_pairs={{0,2},{2,0},{1,3},{3,1},{4,6},{6,4},{5,7},{7,5},{8,10},{10,8},{9,1... | collective-permute-start | bytes 2752520 | tf_op jit(solution)/shard_map/ppermute | solution.py:504
  51.4 6.4 %collective-permute-done.7.refs_0_ = bf16[512,640]{1,0:T(8,128)(2,1)S(1)} collective-permute-done((bf16[512,640]{1,0:T(8,128)(2,1)S(1)}, bf16[512,640]{1,0:T(8,128)(2,1)S(1)}, u32[]{:S(2)}, u32[]{:S(2)}) %collective-permute-start.7) | collective-permute-done | bytes 655392 | tf_op jit(solution)/shard_map/ppermute | solution.py:494
  57.9 4.4 %project.1.refs_0_.terms = bf16[512,2560]{1,0:T(8,128)(2,1)S(1)} custom-call(bf16[512,640]{1,0:T(8,128)(2,1)S(1)} %near.1.rest_0_.mine, bf16[512,640]{1,0:T(8,128)(2,1)S(1)} %collective-permute-done.6.other, bf16[1280,2560]{1,0:T(8,128)(2,1)S(1)} %get-tuple-element.27.refs_3_.weight, bf16[512,640]{1,0:T(8,128)(2,1)S(1)} %gate.1.rest_0_.refs_1_.mine), custom_call_target="tpu_custom_call" | custom-call | flops 1024 | bytes 1024 | tf_op jit(solution)/shard_map/project/pallas_call | solution.py:385
  62.2 2.1 %add_remote.3.total = bf16[512,2560]{1,0:T(8,128)(2,1)} custom-call(bf16[512,2560]{1,0:T(8,128)(2,1)S(1)} %project.1.refs_0_.terms, bf16[512,640]{1,0:T(8,128)(2,1)S(1)} %gate.1.rest_0_.refs_1_.mine, bf16[512,640]{1,0:T(8,128)(2,1)S(1)} %collective-permute-done.10.refs_2_.other, bf16[1280,640]{1,0:T(8,128)(2,1)S(1)} %collective-permute-done.5.array.refs_3_), custom_call_target="tpu_custom_call" | custom-call | flops 1024 | bytes 1024 | tf_op jit(solution)/shard_map/add_remote/pallas_call | solution.py:442
  64.3 8.5 %collective-permute-done.12.weight = bf16[1280,512]{1,0:T(8,128)(2,1)S(1)} collective-permute-done((bf16[1280,512]{1,0:T(8,128)(2,1)S(1)}, bf16[1280,512]{1,0:T(8,128)(2,1)S(1)}, u32[]{:S(2)}, u32[]{:S(2)}) %collective-permute-start.12) | collective-permute-done | bytes 1310752 | tf_op jit(solution)/shard_map/ppermute | solution.py:497
  72.9 1.7 %add_remote.4.total = bf16[512,2560]{1,0:T(8,128)(2,1)} custom-call(bf16[512,2560]{1,0:T(8,128)(2,1)S(1)} %project.1.refs_0_.terms, bf16[512,640]{1,0:T(8,128)(2,1)S(1)} %gate.1.rest_0_.refs_1_.mine, bf16[512,640]{1,0:T(8,128)(2,1)S(1)} %collective-permute-done.10.refs_2_.other, ...), custom_call_target="tpu_custom_call", output_to_operand_aliasing={{}: (4, {})} | custom-call | flops 1024 | bytes 1024 | tf_op jit(solution)/shard_map/add_remote/pallas_call | solution.py:442
  74.6 1.7 %add_remote.5.total = bf16[512,2560]{1,0:T(8,128)(2,1)} custom-call(bf16[512,2560]{1,0:T(8,128)(2,1)S(1)} %project.1.refs_0_.terms, bf16[512,640]{1,0:T(8,128)(2,1)S(1)} %gate.1.rest_0_.refs_1_.mine, bf16[512,640]{1,0:T(8,128)(2,1)S(1)} %collective-permute-done.10.refs_2_.other, ...), custom_call_target="tpu_custom_call", output_to_operand_aliasing={{}: (4, {})} | custom-call | flops 1024 | bytes 1024 | tf_op jit(solution)/shard_map/add_remote/pallas_call | solution.py:442
  76.7 1.1 %add_unshared.1 = bf16[512,2560]{1,0:T(8,128)(2,1)} custom-call(bf16[512,2560]{1,0:T(8,128)(2,1)S(1)} %project.1.refs_0_.terms, bf16[512,896]{1,0:T(8,128)(2,1)S(1)} %collective-permute-done.9.came, bf16[512,2560]{1,0:T(8,128)(2,1)} %add_remote.5.total), custom_call_target="tpu_custom_call", output_to_operand_aliasing={{}: (2, {})} | custom-call | flops 1024 | bytes 1024 | tf_op jit(solution)/shard_map/add_unshared/pallas_call | solution.py:442
  (17 shorter events, 1.8 us)
Async XLA Ops:
  2.7 7.3 %collective-permute-start = (bf16[1152,640]{1,0:T(8,128)(2,1)S(1)}, bf16[1152,640]{1,0:T(8,128)(2,1)S(1)}, u32[]{:S(2)}, u32[]{:S(2)}) collective-permute-start(bf16[1152,640]{1,0:T(8,128)(2,1)S(1)} %get-tuple-element.18), channel_id=1, source_target_pairs={{0,1},{1,0},{2,3},{3,2},{4,5},{5,4},{6,7},{7,6},{8,9},{9,8},{10,11... | collective-permute-start | bytes 4423688 | tf_op jit(solution)/shard_map/ppermute | solution.py:483
  3.2 39.0 %collective-permute-start.5 = (bf16[1280,640]{1,0:T(8,128)(2,1)S(1)}, bf16[1280,640]{1,0:T(8,128)(2,1)S(1)}, u32[]{:S(2)}, u32[]{:S(2)}) collective-permute-start(bf16[1280,640]{1,0:T(8,128)(2,1)S(1)} %get-tuple-element.28), channel_id=1, source_target_pairs={{0,2},{2,0},{1,3},{3,1},{4,6},{6,4},{5,7},{7,5},{8,10},{10,8},{9,1... | collective-permute-start | bytes 4915208 | tf_op jit(solution)/shard_map/ppermute | solution.py:482
  5.8 25.5 %collective-permute-start.1 = (bf16[256,640]{1,0:T(8,128)(2,1)S(1)}, bf16[256,640]{1,0:T(8,128)(2,1)S(1)}, u32[]{:S(2)}, u32[]{:S(2)}) collective-permute-start(bf16[256,640]{1,0:T(8,128)(2,1)S(1)} %get-tuple-element.24), channel_id=1, source_target_pairs={{0,8},{1,13},{4,12},{5,9},{8,0},{9,5},{12,4},{13,1},{2,10},{3,15},... | collective-permute-start | bytes 983048 | tf_op jit(solution)/shard_map/ppermute | solution.py:481
  8.4 22.9 %collective-permute-start.2 = (bf16[256,640]{1,0:T(8,128)(2,1)S(1)}, bf16[256,640]{1,0:T(8,128)(2,1)S(1)}, u32[]{:S(2)}, u32[]{:S(2)}) collective-permute-start(bf16[256,640]{1,0:T(8,128)(2,1)S(1)} %get-tuple-element.25), channel_id=1, source_target_pairs={{0,12},{1,9},{4,8},{5,13},{8,4},{9,1},{12,0},{13,5},{2,14},{3,11},... | collective-permute-start | bytes 983048 | tf_op jit(solution)/shard_map/ppermute | solution.py:481
  9.7 21.5 %collective-permute-start.3 = (bf16[256,640]{1,0:T(8,128)(2,1)S(1)}, bf16[256,640]{1,0:T(8,128)(2,1)S(1)}, u32[]{:S(2)}, u32[]{:S(2)}) collective-permute-start(bf16[256,640]{1,0:T(8,128)(2,1)S(1)} %get-tuple-element.26), channel_id=1, source_target_pairs={{0,4},{1,5},{4,0},{5,1},{8,12},{9,13},{12,8},{13,9},{2,6},{3,7},{6... | collective-permute-start | bytes 983048 | tf_op jit(solution)/shard_map/ppermute | solution.py:481
  31.3 7.1 %collective-permute-start.4 = (bf16[384,640]{1,0:T(8,128)(2,1)S(1)}, bf16[384,640]{1,0:T(8,128)(2,1)S(1)}, u32[]{:S(2)}, u32[]{:S(2)}) collective-permute-start(bf16[384,640]{1,0:T(8,128)(2,1)S(1)} %pass_on.1.rest_4_), channel_id=1, source_target_pairs={{0,1},{1,0},{2,3},{3,2},{4,5},{5,4},{6,7},{7,6},{8,9},{9,8},{10,11... | collective-permute-start | bytes 1474568 | tf_op jit(solution)/shard_map/ppermute | solution.py:488
  39.8 8.0 %collective-permute-start.8 = (bf16[512,640]{1,0:T(8,128)(2,1)S(1)}, bf16[512,640]{1,0:T(8,128)(2,1)S(1)}, u32[]{:S(2)}, u32[]{:S(2)}) collective-permute-start(bf16[512,640]{1,0:T(8,128)(2,1)S(1)} %far_last.1.after.mine), channel_id=1, source_target_pairs={{0,1},{1,0},{2,3},{3,2},{4,5},{5,4},{6,7},{7,6},{8,9},{9,8},{10,11... | collective-permute-start | bytes 1966088 | tf_op jit(solution)/shard_map/ppermute | solution.py:495
  40.3 17.6 %collective-permute-start.7 = (bf16[512,640]{1,0:T(8,128)(2,1)S(1)}, bf16[512,640]{1,0:T(8,128)(2,1)S(1)}, u32[]{:S(2)}, u32[]{:S(2)}) collective-permute-start(bf16[512,640]{1,0:T(8,128)(2,1)S(1)} %far_last.1.after.mine), channel_id=1, source_target_pairs={{0,2},{2,0},{1,3},{3,1},{4,6},{6,4},{5,7},{7,5},{8,10},{10,8},{9,1... | collective-permute-start | bytes 1966088 | tf_op jit(solution)/shard_map/ppermute | solution.py:494
  42.3 30.6 %collective-permute-start.12 = (bf16[1280,512]{1,0:T(8,128)(2,1)S(1)}, bf16[1280,512]{1,0:T(8,128)(2,1)S(1)}, u32[]{:S(2)}, u32[]{:S(2)}) collective-permute-start(bf16[1280,512]{1,0:T(8,128)(2,1)S(1)} %leading.1.rest_8_), channel_id=1, source_target_pairs={{0,16},{16,0},{1,17},{17,1},{2,18},{18,2},{3,19},{19,3},{4,20},{20... | collective-permute-start | bytes 3932168 | tf_op jit(solution)/shard_map/ppermute | solution.py:497
  44.1 30.5 %collective-permute-start.11 = (bf16[1280,512]{1,0:T(8,128)(2,1)S(1)}, bf16[1280,512]{1,0:T(8,128)(2,1)S(1)}, u32[]{:S(2)}, u32[]{:S(2)}) collective-permute-start(bf16[1280,512]{1,0:T(8,128)(2,1)S(1)} %leading.1.rest_8_), channel_id=1, source_target_pairs={{0,4},{4,0},{8,12},{12,8},{1,5},{5,1},{9,13},{13,9},{2,6},{6,2},{1... | collective-permute-start | bytes 3932168 | tf_op jit(solution)/shard_map/ppermute | solution.py:498
  49.7 27.0 %collective-permute-start.9 = (bf16[512,896]{1,0:T(8,128)(2,1)S(1)}, bf16[512,896]{1,0:T(8,128)(2,1)S(1)}, u32[]{:S(2)}, u32[]{:S(2)}) collective-permute-start(bf16[512,896]{1,0:T(8,128)(2,1)S(1)} %project_unshared.1.refs_1_), channel_id=1, source_target_pairs={{0,2},{2,0},{1,3},{3,1},{4,6},{6,4},{5,7},{7,5},{8,10},{10,8},{9,1... | collective-permute-start | bytes 2752520 | tf_op jit(solution)/shard_map/ppermute | solution.py:504
  51.4 6.4 %collective-permute-start.6 = (bf16[512,640]{1,0:T(8,128)(2,1)S(1)}, bf16[512,640]{1,0:T(8,128)(2,1)S(1)}, u32[]{:S(2)}, u32[]{:S(2)}) collective-permute-start(bf16[512,640]{1,0:T(8,128)(2,1)S(1)} %near.1.rest_0_.mine), channel_id=1, source_target_pairs={{0,1},{1,0},{2,3},{3,2},{4,5},{5,4},{6,7},{7,6},{8,9},{9,8},{10,11... | collective-permute-start | bytes 1966088 | tf_op jit(solution)/shard_map/ppermute | solution.py:501
  57.8 4.4 %collective-permute-start.10 = (bf16[512,640]{1,0:T(8,128)(2,1)S(1)}, bf16[512,640]{1,0:T(8,128)(2,1)S(1)}, u32[]{:S(2)}, u32[]{:S(2)}) collective-permute-start(bf16[512,640]{1,0:T(8,128)(2,1)S(1)} %gate.1.rest_0_.refs_1_.mine), channel_id=1, source_target_pairs={{0,1},{1,0},{2,3},{3,2},{4,5},{5,4},{6,7},{7,6},{8,9},{9,8},{10,11... | collective-permute-start | bytes 1966088 | tf_op jit(solution)/shard_map/ppermute | solution.py:506

commit v4 on v3

--- a/solution.py
+++ b/solution.py
@@ -118,7 +118,7 @@
 
 
 def pack(frame_ids, mem_keys, mem_values, cur_keys, cur_values, weight, low, share, seq_count):
-    parts = 4
+    parts = 2
     width = mem_keys.shape[2] // 2
     rows = [2 * FT] + [4 * FT] * (seq_count - 1) + [2 * cur_keys.shape[0] + 2 * FT]
     shapes = [(count, width) for count in rows] + [(weight.shape[0], share)]
@@ -353,6 +353,22 @@
     )
 
 
+def side_by_side_kernel(mine, other, out):
+    out[...] = both(mine, other)
+
+
+def side_by_side(mine, other):
+    return pl.pallas_call(
+        side_by_side_kernel,
+        in_specs=[VMEM] * 2,
+        out_specs=VMEM,
+        out_shape=pltpu.VMEM((mine.shape[0], 2 * mine.shape[1]), BF16),
+        compiler_params=params(),
+        name="side_by_side",
+        cost_estimate=SHORT,
+    )(in_vmem(mine), in_vmem(other))
+
+
 def project_kernel(step, mine, other, weight, *rest):
     out = rest[-1]
     rows = both(mine, other)
@@ -416,10 +432,10 @@
         copy.wait()
 
 
-def remote_kernel(first, share, other_seq, other_group, terms, mine, other, weight, total, out, scratch, sems):
+def remote_kernel(first, share, other_seq, other_group, terms, rows, weight, total, out, scratch, sems):
     block = weight.shape[1]
     low = pl.multiple_of(first + quarter(other_seq, other_group) * share, 128)
-    product = jnp.dot(both(mine, other), weight[...], preferred_element_type=F32)
+    product = jnp.dot(rows[...], weight[...], preferred_element_type=F32)
     write_blocks([(terms[:, pl.ds(low, block)].astype(F32) + product, low)], out, scratch, sems)
 
 
@@ -452,9 +468,9 @@
     )(*map(in_vmem, operands), *totals)
 
 
-def add_remote(terms, mine, other, weight, first, share, other_seq, other_group, total):
+def add_remote(terms, rows, weight, first, share, other_seq, other_group, total):
     kernel = functools.partial(remote_kernel, first, share, other_seq, other_group)
-    return finish_block(kernel, "add_remote", (terms, mine, other, weight), total, *terms.shape, weight.shape[1])
+    return finish_block(kernel, "add_remote", (terms, rows, weight), total, *terms.shape, weight.shape[1])
 
 
 def add_unshared(terms, came, low, share, passed, total):
@@ -506,7 +522,7 @@
     came_other = lax.ppermute(came_mine, "sub", SWAP)
     terms = project(near, near_sibling, weight, (came_mine,))
 
-    arrived = (terms, came_mine, came_other)
+    arrived = (terms, side_by_side(came_mine, came_other))
     total = add_remote(*arrived, columns, low, share, False, False, None)
     total = add_remote(*arrived, group_columns, low, share, False, True, total)
     total = add_remote(*arrived, seq_columns, low, share, True, False, total)

time: 78 us -> 77.9 us (level)
  transfers between devices with their start and end apart: 13 -> 13, of which waited for: 6 -> 5; matrix products, arithmetic and copies ran while one was open for 0% -> 0% of each run, Pallas kernels for 41% -> 41%
where the time goes in v4:
time: 77.9 us; the launch traced here: 77.7 us
  Pallas kernels  35.5 us (46%)
  waiting for transfers between devices  22.8 us (29%)
  starting transfers between devices  19.3 us (25%)
    pallas_call x1, Pallas kernels, attend_current(): pl.pallas_call(functools.partial(current_kernel, 512), in_specs=[HBM] * 3...  11.3 us
    ppermute x1, waiting for transfers between devices, local(): group_columns = lax.ppermute(columns_copy, 'groups', SWAP)  8.39 us
    pallas_call x4, Pallas kernels, finish_block(): pl.pallas_call(body, in_specs=[VMEM] * count + [HBM] * len(totals), out_s...  6.54 us
    ppermute x1, waiting for transfers between devices, local(): came_mine = lax.ppermute(far, 'head', SWAP)  6.5 us
    ppermute x3, waiting for transfers between devices, local(): mine.append(lax.ppermute(sends[place], ('seq', 'sub'), pairs))  6.37 us
    pallas_call x2, Pallas kernels, project_call(): pl.pallas_call(kernel, in_specs=[VMEM] * 3 + [ANY] * len(after), out_spec...  6.28 us
    ppermute x1, starting transfers between devices, local(): theirs = lax.ppermute(passed, 'sub', SWAP)  5.61 us
    pallas_call x3, Pallas kernels, attend_frames(): pl.pallas_call(functools.partial(frames_kernel, heads, half, state_half,...  4.94 us
  transfers between devices with their start and end apart: 13, of which 5 were waited for; matrix products, arithmetic and copies ran while one was open for 0% of the time, Pallas kernels for 41%

profile of v4, /device:TPU:0, one launch (start us, length us, event | category | flops | bytes accessed | tf_op | source)
XLA Modules:
  0.0 77.7 jit_solution(17090010980111294229)
XLA Ops:
  0.0 2.5 %pack.1 = (bf16[128,640]{1,0:T(8,128)(2,1)S(1)}, bf16[256,640]{1,0:T(8,128)(2,1)S(1)}, bf16[256,640]{1,0:T(8,128)(2,1)S(1)}, bf16[256,640]{1,0:T(8,128)(2,1)S(1)...) custom-call(s32[4,8]{1,0:T(4,128)} %ids.1, bf16[16,64,1280]{2,1,0:T(8,128)(2,1)} %keys.1, ...), custom_call_target="tpu_custom_call" | custom-call | bytes 12582912 | tf_op jit(solution)/shard_map/pack/pallas_call | solution.py:125
  3.1 2.6 %collective-permute-start.5 = (bf16[1280,640]{1,0:T(8,128)(2,1)S(1)}, bf16[1280,640]{1,0:T(8,128)(2,1)S(1)}, u32[]{:S(2)}, u32[]{:S(2)}) collective-permute-start(bf16[1280,640]{1,0:T(8,128)(2,1)S(1)} %get-tuple-element.28), channel_id=1, source_target_pairs={{0,2},{2,0},{1,3},{3,1},{4,6},{6,4},{5,7},{7,5},{8,10},{10,8},{9,1... | collective-permute-start | bytes 4915208 | tf_op jit(solution)/shard_map/ppermute | solution.py:498
  5.6 2.6 %collective-permute-start.1 = (bf16[256,640]{1,0:T(8,128)(2,1)S(1)}, bf16[256,640]{1,0:T(8,128)(2,1)S(1)}, u32[]{:S(2)}, u32[]{:S(2)}) collective-permute-start(bf16[256,640]{1,0:T(8,128)(2,1)S(1)} %get-tuple-element.24), channel_id=1, source_target_pairs={{0,8},{1,13},{4,12},{5,9},{8,0},{9,5},{12,4},{13,1},{2,10},{3,15},... | collective-permute-start | bytes 983048 | tf_op jit(solution)/shard_map/ppermute | solution.py:497
  8.2 1.3 %collective-permute-start.2 = (bf16[256,640]{1,0:T(8,128)(2,1)S(1)}, bf16[256,640]{1,0:T(8,128)(2,1)S(1)}, u32[]{:S(2)}, u32[]{:S(2)}) collective-permute-start(bf16[256,640]{1,0:T(8,128)(2,1)S(1)} %get-tuple-element.25), channel_id=1, source_target_pairs={{0,12},{1,9},{4,8},{5,13},{8,4},{9,1},{12,0},{13,5},{2,14},{3,11},... | collective-permute-start | bytes 983048 | tf_op jit(solution)/shard_map/ppermute | solution.py:497
  9.8 11.3 %attend_current.1 = (f32[5,1024,128]{2,1,0:T(8,128)S(1)}, f32[5,1024,128]{2,1,0:T(8,128)S(1)}, bf16[1024,640]{1,0:T(8,128)(2,1)S(1)}) custom-call(bf16[1024,1280]{1,0:T(8,128)(2,1)} %queries.1, bf16[512,1280]{1,0:T(8,128)(2,1)} %own_keys.1, bf16[512,1280]{1,0:T(8,128)(2,1)} %own_values.1, bf16[1152,640]{1,0:T(8,128)(2,1)S(1)} %collective-permute-done.sibling.rest_0_.rest_4_), custom_call_target="tpu_custom_call" | custom-call | flops 4026531840 | bytes 7864320 | tf_op jit(solution)/shard_map/attend_current/pallas_call | solution.py:262
  21.1 3.6 %load.1 = (bf16[1280,2560]{1,0:T(8,128)(2,1)S(1)}, f32[8,64]{1,0:T(8,128)S(1)}) custom-call(s32[4,8]{1,0:T(4,128)} %ids.1, s32[128]{0:T(128)} %counts.1, bf16[1280,2560]{1,0:T(8,128)(2,1)} %weight.3, f32[5,1024,128]{2,1,0:T(8,128)S(1)} %get-tuple-element.19.after.lse), custom_call_target="tpu_custom_call" | custom-call | bytes 6553600 | tf_op jit(solution)/shard_map/load/pallas_call | solution.py:181
  24.7 6.4 %collective-permute-done.1.refs_0_.rest_1_ = bf16[256,640]{1,0:T(8,128)(2,1)S(1)} collective-permute-done((bf16[256,640]{1,0:T(8,128)(2,1)S(1)}, bf16[256,640]{1,0:T(8,128)(2,1)S(1)}, u32[]{:S(2)}, u32[]{:S(2)}) %collective-permute-start.1) | collective-permute-done | bytes 327712 | tf_op jit(solution)/shard_map/ppermute | solution.py:497
  31.2 5.6 %collective-permute-start.4 = (bf16[384,640]{1,0:T(8,128)(2,1)S(1)}, bf16[384,640]{1,0:T(8,128)(2,1)S(1)}, u32[]{:S(2)}, u32[]{:S(2)}) collective-permute-start(bf16[384,640]{1,0:T(8,128)(2,1)S(1)} %pass_on.1.rest_4_), channel_id=1, source_target_pairs={{0,1},{1,0},{2,3},{3,2},{4,5},{5,4},{6,7},{7,6},{8,9},{9,8},{10,11... | collective-permute-start | bytes 1474568 | tf_op jit(solution)/shard_map/ppermute | solution.py:504
  36.8 1.4 %far_first.1 = (f32[5,512,128]{2,1,0:T(8,128)S(1)}, f32[5,512,128]{2,1,0:T(8,128)S(1)}) custom-call(f32[8,64]{1,0:T(8,128)S(1)} %get-tuple-element.20.bias, bf16[1024,640]{1,0:T(8,128)(2,1)S(1)} %get-tuple-element.21.q, f32[5,1024,128]{2,1,0:T(8,128)S(1)} %get-tuple-element.22.held, f32[5,1024,128]{2,1,0:T(8,128)S(1)} %get-tuple-element.19.after.lse, ...), custom_call_target="tpu_custom_call" | custom-call | flops 1024 | bytes 1024 | tf_op jit(solution)/shard_map/far_first/pallas_call | solution.py:335
  38.3 1.4 %far_last.1.after.mine = bf16[512,640]{1,0:T(8,128)(2,1)S(1)} custom-call(f32[8,64]{1,0:T(8,128)S(1)} %get-tuple-element.20.bias, bf16[1024,640]{1,0:T(8,128)(2,1)S(1)} %get-tuple-element.21.q, f32[5,512,128]{2,1,0:T(8,128)S(1)} %get-tuple-element.29.held, f32[5,512,128]{2,1,0:T(8,128)S(1)} %get-tuple-element.30.lse, ...), custom_call_target="tpu_custom_call" | custom-call | flops 1024 | bytes 1024 | tf_op jit(solution)/shard_map/far_last/pallas_call | solution.py:335
  40.1 0.9 %collective-permute-start.7 = (bf16[512,640]{1,0:T(8,128)(2,1)S(1)}, bf16[512,640]{1,0:T(8,128)(2,1)S(1)}, u32[]{:S(2)}, u32[]{:S(2)}) collective-permute-start(bf16[512,640]{1,0:T(8,128)(2,1)S(1)} %far_last.1.after.mine), channel_id=1, source_target_pairs={{0,2},{2,0},{1,3},{3,1},{4,6},{6,4},{5,7},{7,5},{8,10},{10,8},{9,1... | collective-permute-start | bytes 1966088 | tf_op jit(solution)/shard_map/ppermute | solution.py:510
  41.0 1.0 %collective-permute-done.5.array.refs_2_ = bf16[1280,640]{1,0:T(8,128)(2,1)S(1)} collective-permute-done((bf16[1280,640]{1,0:T(8,128)(2,1)S(1)}, bf16[1280,640]{1,0:T(8,128)(2,1)S(1)}, u32[]{:S(2)}, u32[]{:S(2)}) %collective-permute-start.5) | collective-permute-done | bytes 1638432 | tf_op jit(solution)/shard_map/ppermute | solution.py:498
  42.1 1.9 %collective-permute-start.12 = (bf16[1280,512]{1,0:T(8,128)(2,1)S(1)}, bf16[1280,512]{1,0:T(8,128)(2,1)S(1)}, u32[]{:S(2)}, u32[]{:S(2)}) collective-permute-start(bf16[1280,512]{1,0:T(8,128)(2,1)S(1)} %leading.1.rest_8_), channel_id=1, source_target_pairs={{0,16},{16,0},{1,17},{17,1},{2,18},{18,2},{3,19},{19,3},{4,20},{20... | collective-permute-start | bytes 3932168 | tf_op jit(solution)/shard_map/ppermute | solution.py:513
  44.0 1.6 %collective-permute-start.11 = (bf16[1280,512]{1,0:T(8,128)(2,1)S(1)}, bf16[1280,512]{1,0:T(8,128)(2,1)S(1)}, u32[]{:S(2)}, u32[]{:S(2)}) collective-permute-start(bf16[1280,512]{1,0:T(8,128)(2,1)S(1)} %leading.1.rest_8_), channel_id=1, source_target_pairs={{0,4},{4,0},{8,12},{12,8},{1,5},{5,1},{9,13},{13,9},{2,6},{6,2},{1... | collective-permute-start | bytes 3932168 | tf_op jit(solution)/shard_map/ppermute | solution.py:514
  45.5 2.1 %near.1.rest_0_.mine = bf16[512,640]{1,0:T(8,128)(2,1)S(1)} custom-call(f32[8,64]{1,0:T(8,128)S(1)} %get-tuple-element.20.bias, bf16[1024,640]{1,0:T(8,128)(2,1)S(1)} %get-tuple-element.21.q, f32[5,1024,128]{2,1,0:T(8,128)S(1)} %get-tuple-element.22.held, f32[5,1024,128]{2,1,0:T(8,128)S(1)} %get-tuple-element.19.after.lse, ...), custom_call_target="tpu_custom_call" | custom-call | flops 1024 | bytes 1024 | tf_op jit(solution)/shard_map/near/pallas_call | solution.py:335
  47.6 1.9 %project_unshared.1.refs_1_ = bf16[512,896]{1,0:T(8,128)(2,1)S(1)} custom-call(bf16[512,640]{1,0:T(8,128)(2,1)S(1)} %far_last.1.after.mine, bf16[512,640]{1,0:T(8,128)(2,1)S(1)} %collective-permute-done.8.other, bf16[1280,2560]{1,0:T(8,128)(2,1)S(1)} %get-tuple-element.27.refs_3_.weight, bf16[512,640]{1,0:T(8,128)(2,1)S(1)} %near.1.rest_0_.mine), custom_call_target="tpu_custom_call" | custom-call | flops 1024 | bytes 1024 | tf_op jit(solution)/shard_map/project_unshared/pallas_call | solution.py:401
  49.5 1.7 %collective-permute-start.9 = (bf16[512,896]{1,0:T(8,128)(2,1)S(1)}, bf16[512,896]{1,0:T(8,128)(2,1)S(1)}, u32[]{:S(2)}, u32[]{:S(2)}) collective-permute-start(bf16[512,896]{1,0:T(8,128)(2,1)S(1)} %project_unshared.1.refs_1_), channel_id=1, source_target_pairs={{0,2},{2,0},{1,3},{3,1},{4,6},{6,4},{5,7},{7,5},{8,10},{10,8},{9,1... | collective-permute-start | bytes 2752520 | tf_op jit(solution)/shard_map/ppermute | solution.py:520
  51.2 6.5 %collective-permute-done.7.refs_0_ = bf16[512,640]{1,0:T(8,128)(2,1)S(1)} collective-permute-done((bf16[512,640]{1,0:T(8,128)(2,1)S(1)}, bf16[512,640]{1,0:T(8,128)(2,1)S(1)}, u32[]{:S(2)}, u32[]{:S(2)}) %collective-permute-start.7) | collective-permute-done | bytes 655392 | tf_op jit(solution)/shard_map/ppermute | solution.py:510
  57.7 4.4 %project.1.refs_0_.terms = bf16[512,2560]{1,0:T(8,128)(2,1)S(1)} custom-call(bf16[512,640]{1,0:T(8,128)(2,1)S(1)} %near.1.rest_0_.mine, bf16[512,640]{1,0:T(8,128)(2,1)S(1)} %collective-permute-done.6.other, bf16[1280,2560]{1,0:T(8,128)(2,1)S(1)} %get-tuple-element.27.refs_3_.weight, bf16[512,640]{1,0:T(8,128)(2,1)S(1)} %gate.1.rest_0_.mine), custom_call_target="tpu_custom_call" | custom-call | flops 1024 | bytes 1024 | tf_op jit(solution)/shard_map/project/pallas_call | solution.py:401
  62.2 2.1 %add_remote.3.total = bf16[512,2560]{1,0:T(8,128)(2,1)} custom-call(bf16[512,2560]{1,0:T(8,128)(2,1)S(1)} %project.1.refs_0_.terms, bf16[512,1280]{1,0:T(8,128)(2,1)S(1)} %side_by_side.1.refs_1_.rows, bf16[1280,640]{1,0:T(8,128)(2,1)S(1)} %collective-permute-done.5.array.refs_2_), custom_call_target="tpu_custom_call" | custom-call | flops 1024 | bytes 1024 | tf_op jit(solution)/shard_map/add_remote/pallas_call | solution.py:458
  64.3 8.4 %collective-permute-done.12.weight = bf16[1280,512]{1,0:T(8,128)(2,1)S(1)} collective-permute-done((bf16[1280,512]{1,0:T(8,128)(2,1)S(1)}, bf16[1280,512]{1,0:T(8,128)(2,1)S(1)}, u32[]{:S(2)}, u32[]{:S(2)}) %collective-permute-start.12) | collective-permute-done | bytes 1310752 | tf_op jit(solution)/shard_map/ppermute | solution.py:513
  72.7 1.7 %add_remote.4.total = bf16[512,2560]{1,0:T(8,128)(2,1)} custom-call(bf16[512,2560]{1,0:T(8,128)(2,1)S(1)} %project.1.refs_0_.terms, bf16[512,1280]{1,0:T(8,128)(2,1)S(1)} %side_by_side.1.refs_1_.rows, bf16[1280,512]{1,0:T(8,128)(2,1)S(1)} %collective-permute-done.12.weight, bf16[512,2560]{1,0:T(8,128)(2,1)} %add_remote.3.total), custom_call_target="tpu_custom_call", output_to_operand_aliasing={{}: (3, {})} | custom-call | flops 1024 | bytes 1024 | tf_op jit(solution)/shard_map/add_remote/pallas_call | solution.py:458
  74.4 1.7 %add_remote.5.total = bf16[512,2560]{1,0:T(8,128)(2,1)} custom-call(bf16[512,2560]{1,0:T(8,128)(2,1)S(1)} %project.1.refs_0_.terms, bf16[512,1280]{1,0:T(8,128)(2,1)S(1)} %side_by_side.1.refs_1_.rows, bf16[1280,512]{1,0:T(8,128)(2,1)S(1)} %collective-permute-done.11.weight, bf16[512,2560]{1,0:T(8,128)(2,1)} %add_remote.4.total), custom_call_target="tpu_custom_call", output_to_operand_aliasing={{}: (3, {})} | custom-call | flops 1024 | bytes 1024 | tf_op jit(solution)/shard_map/add_remote/pallas_call | solution.py:458
  76.6 1.1 %add_unshared.1 = bf16[512,2560]{1,0:T(8,128)(2,1)} custom-call(bf16[512,2560]{1,0:T(8,128)(2,1)S(1)} %project.1.refs_0_.terms, bf16[512,896]{1,0:T(8,128)(2,1)S(1)} %collective-permute-done.9.came, bf16[512,2560]{1,0:T(8,128)(2,1)} %add_remote.5.total), custom_call_target="tpu_custom_call", output_to_operand_aliasing={{}: (2, {})} | custom-call | flops 1024 | bytes 1024 | tf_op jit(solution)/shard_map/add_unshared/pallas_call | solution.py:458
  (18 shorter events, 2.0 us)
Async XLA Ops:
  2.5 7.3 %collective-permute-start = (bf16[1152,640]{1,0:T(8,128)(2,1)S(1)}, bf16[1152,640]{1,0:T(8,128)(2,1)S(1)}, u32[]{:S(2)}, u32[]{:S(2)}) collective-permute-start(bf16[1152,640]{1,0:T(8,128)(2,1)S(1)} %get-tuple-element.18), channel_id=1, source_target_pairs={{0,1},{1,0},{2,3},{3,2},{4,5},{5,4},{6,7},{7,6},{8,9},{9,8},{10,11... | collective-permute-start | bytes 4423688 | tf_op jit(solution)/shard_map/ppermute | solution.py:499
  3.1 39.0 %collective-permute-start.5 = (bf16[1280,640]{1,0:T(8,128)(2,1)S(1)}, bf16[1280,640]{1,0:T(8,128)(2,1)S(1)}, u32[]{:S(2)}, u32[]{:S(2)}) collective-permute-start(bf16[1280,640]{1,0:T(8,128)(2,1)S(1)} %get-tuple-element.28), channel_id=1, source_target_pairs={{0,2},{2,0},{1,3},{3,1},{4,6},{6,4},{5,7},{7,5},{8,10},{10,8},{9,1... | collective-permute-start | bytes 4915208 | tf_op jit(solution)/shard_map/ppermute | solution.py:498
  5.6 25.5 %collective-permute-start.1 = (bf16[256,640]{1,0:T(8,128)(2,1)S(1)}, bf16[256,640]{1,0:T(8,128)(2,1)S(1)}, u32[]{:S(2)}, u32[]{:S(2)}) collective-permute-start(bf16[256,640]{1,0:T(8,128)(2,1)S(1)} %get-tuple-element.24), channel_id=1, source_target_pairs={{0,8},{1,13},{4,12},{5,9},{8,0},{9,5},{12,4},{13,1},{2,10},{3,15},... | collective-permute-start | bytes 983048 | tf_op jit(solution)/shard_map/ppermute | solution.py:497
  8.2 22.9 %collective-permute-start.2 = (bf16[256,640]{1,0:T(8,128)(2,1)S(1)}, bf16[256,640]{1,0:T(8,128)(2,1)S(1)}, u32[]{:S(2)}, u32[]{:S(2)}) collective-permute-start(bf16[256,640]{1,0:T(8,128)(2,1)S(1)} %get-tuple-element.25), channel_id=1, source_target_pairs={{0,12},{1,9},{4,8},{5,13},{8,4},{9,1},{12,0},{13,5},{2,14},{3,11},... | collective-permute-start | bytes 983048 | tf_op jit(solution)/shard_map/ppermute | solution.py:497
  9.6 21.5 %collective-permute-start.3 = (bf16[256,640]{1,0:T(8,128)(2,1)S(1)}, bf16[256,640]{1,0:T(8,128)(2,1)S(1)}, u32[]{:S(2)}, u32[]{:S(2)}) collective-permute-start(bf16[256,640]{1,0:T(8,128)(2,1)S(1)} %get-tuple-element.26), channel_id=1, source_target_pairs={{0,4},{1,5},{4,0},{5,1},{8,12},{9,13},{12,8},{13,9},{2,6},{3,7},{6... | collective-permute-start | bytes 983048 | tf_op jit(solution)/shard_map/ppermute | solution.py:497
  31.2 7.1 %collective-permute-start.4 = (bf16[384,640]{1,0:T(8,128)(2,1)S(1)}, bf16[384,640]{1,0:T(8,128)(2,1)S(1)}, u32[]{:S(2)}, u32[]{:S(2)}) collective-permute-start(bf16[384,640]{1,0:T(8,128)(2,1)S(1)} %pass_on.1.rest_4_), channel_id=1, source_target_pairs={{0,1},{1,0},{2,3},{3,2},{4,5},{5,4},{6,7},{7,6},{8,9},{9,8},{10,11... | collective-permute-start | bytes 1474568 | tf_op jit(solution)/shard_map/ppermute | solution.py:504
  39.7 7.9 %collective-permute-start.8 = (bf16[512,640]{1,0:T(8,128)(2,1)S(1)}, bf16[512,640]{1,0:T(8,128)(2,1)S(1)}, u32[]{:S(2)}, u32[]{:S(2)}) collective-permute-start(bf16[512,640]{1,0:T(8,128)(2,1)S(1)} %far_last.1.after.mine), channel_id=1, source_target_pairs={{0,1},{1,0},{2,3},{3,2},{4,5},{5,4},{6,7},{7,6},{8,9},{9,8},{10,11... | collective-permute-start | bytes 1966088 | tf_op jit(solution)/shard_map/ppermute | solution.py:511
  40.1 17.6 %collective-permute-start.7 = (bf16[512,640]{1,0:T(8,128)(2,1)S(1)}, bf16[512,640]{1,0:T(8,128)(2,1)S(1)}, u32[]{:S(2)}, u32[]{:S(2)}) collective-permute-start(bf16[512,640]{1,0:T(8,128)(2,1)S(1)} %far_last.1.after.mine), channel_id=1, source_target_pairs={{0,2},{2,0},{1,3},{3,1},{4,6},{6,4},{5,7},{7,5},{8,10},{10,8},{9,1... | collective-permute-start | bytes 1966088 | tf_op jit(solution)/shard_map/ppermute | solution.py:510
  42.1 30.6 %collective-permute-start.12 = (bf16[1280,512]{1,0:T(8,128)(2,1)S(1)}, bf16[1280,512]{1,0:T(8,128)(2,1)S(1)}, u32[]{:S(2)}, u32[]{:S(2)}) collective-permute-start(bf16[1280,512]{1,0:T(8,128)(2,1)S(1)} %leading.1.rest_8_), channel_id=1, source_target_pairs={{0,16},{16,0},{1,17},{17,1},{2,18},{18,2},{3,19},{19,3},{4,20},{20... | collective-permute-start | bytes 3932168 | tf_op jit(solution)/shard_map/ppermute | solution.py:513
  44.0 30.4 %collective-permute-start.11 = (bf16[1280,512]{1,0:T(8,128)(2,1)S(1)}, bf16[1280,512]{1,0:T(8,128)(2,1)S(1)}, u32[]{:S(2)}, u32[]{:S(2)}) collective-permute-start(bf16[1280,512]{1,0:T(8,128)(2,1)S(1)} %leading.1.rest_8_), channel_id=1, source_target_pairs={{0,4},{4,0},{8,12},{12,8},{1,5},{5,1},{9,13},{13,9},{2,6},{6,2},{1... | collective-permute-start | bytes 3932168 | tf_op jit(solution)/shard_map/ppermute | solution.py:514
  49.5 27.1 %collective-permute-start.9 = (bf16[512,896]{1,0:T(8,128)(2,1)S(1)}, bf16[512,896]{1,0:T(8,128)(2,1)S(1)}, u32[]{:S(2)}, u32[]{:S(2)}) collective-permute-start(bf16[512,896]{1,0:T(8,128)(2,1)S(1)} %project_unshared.1.refs_1_), channel_id=1, source_target_pairs={{0,2},{2,0},{1,3},{3,1},{4,6},{6,4},{5,7},{7,5},{8,10},{10,8},{9,1... | collective-permute-start | bytes 2752520 | tf_op jit(solution)/shard_map/ppermute | solution.py:520
  51.2 6.5 %collective-permute-start.6 = (bf16[512,640]{1,0:T(8,128)(2,1)S(1)}, bf16[512,640]{1,0:T(8,128)(2,1)S(1)}, u32[]{:S(2)}, u32[]{:S(2)}) collective-permute-start(bf16[512,640]{1,0:T(8,128)(2,1)S(1)} %near.1.rest_0_.mine), channel_id=1, source_target_pairs={{0,1},{1,0},{2,3},{3,2},{4,5},{5,4},{6,7},{7,6},{8,9},{9,8},{10,11... | collective-permute-start | bytes 1966088 | tf_op jit(solution)/shard_map/ppermute | solution.py:517
  57.7 4.4 %collective-permute-start.10 = (bf16[512,640]{1,0:T(8,128)(2,1)S(1)}, bf16[512,640]{1,0:T(8,128)(2,1)S(1)}, u32[]{:S(2)}, u32[]{:S(2)}) collective-permute-start(bf16[512,640]{1,0:T(8,128)(2,1)S(1)} %gate.1.rest_0_.mine), channel_id=1, source_target_pairs={{0,1},{1,0},{2,3},{3,2},{4,5},{5,4},{6,7},{7,6},{8,9},{9,8},{10,11... | collective-permute-start | bytes 1966088 | tf_op jit(solution)/shard_map/ppermute | solution.py:522

commit v5 on v1

--- a/solution.py
+++ b/solution.py
@@ -417,12 +417,19 @@
 
 
 def add_kernel(low, share, passed, terms, came, total, out, scratch, sems):
-    blocks, start = [], 0
-    for columns in unshared_columns(low, share, passed):
-        block = terms[:, columns].astype(F32) + came[:, pl.ds(start, columns.size)].astype(F32)
-        blocks.append((block, columns.start))
-        start += columns.size
-    write_blocks(blocks, out, scratch, sems)
+    half = came.shape[0] // 2
+    copies = []
+    for row in (0, half):
+        rows, start = pl.ds(row, half), 0
+        for columns in unshared_columns(low, share, passed):
+            span = pl.ds(start, columns.size)
+            scratch[rows, span] = (terms[rows, columns].astype(F32) + came[rows, span].astype(F32)).astype(BF16)
+            copy = pltpu.make_async_copy(scratch.at[rows, span], out.at[rows, columns], sems.at[len(copies)])
+            copy.start()
+            copies.append(copy)
+            start += columns.size
+    for copy in copies:
+        copy.wait()
 
 
 def finish_block(kernel, name, operands, total, rows, width, block):
@@ -438,7 +445,7 @@
         out_specs=HBM,
         out_shape=pltpu.HBM((rows, width), BF16),
         input_output_aliases=aliases,
-        scratch_shapes=[pltpu.VMEM((rows, block), BF16), pltpu.SemaphoreType.DMA((4,))],
+        scratch_shapes=[pltpu.VMEM((rows, block), BF16), pltpu.SemaphoreType.DMA((8,))],
         compiler_params=params(),
         name=name,
         cost_estimate=SHORT,

time: 77.7 us -> 77.7 us (level)
  no operation moved by 1% of the time
where the time goes in v5:
time: 77.7 us; the launch traced here: 77.5 us
  Pallas kernels  35.6 us (46%)
  waiting for transfers between devices  28.9 us (37%)
  starting transfers between devices  12.9 us (17%)
    pallas_call x1, Pallas kernels, attend_current(): pl.pallas_call(functools.partial(current_kernel, 512), in_specs=[HBM] * 3...  11.3 us
    ppermute x1, waiting for transfers between devices, local(): group_columns = lax.ppermute(columns_copy, 'groups', SWAP)  9.84 us
    ppermute x3, waiting for transfers between devices, local(): lax.ppermute(sent, 'seq', [(index, index ^ flip) for index in range(seq_c...  6.97 us
    pallas_call x4, Pallas kernels, finish_block(): pl.pallas_call(body, in_specs=[VMEM] * count + [HBM] * len(totals), out_s...  6.66 us
    ppermute x1, waiting for transfers between devices, local(): columns = lax.ppermute(columns, 'head', SWAP)  6.5 us
    pallas_call x2, Pallas kernels, project_call(): pl.pallas_call(kernel, in_specs=[VMEM] * 3 + [ANY] * len(after), out_spec...  6.28 us
    ppermute x1, waiting for transfers between devices, local(): came_mine = lax.ppermute(far, 'head', SWAP)  5.11 us
    pallas_call x3, Pallas kernels, attend_frames(): pl.pallas_call(functools.partial(frames_kernel, heads, half, state_half,...  4.89 us
  transfers between devices with their start and end apart: 13, of which 6 were waited for; matrix products, arithmetic and copies ran while one was open for 0% of the time, Pallas kernels for 41%

profile of v5, /device:TPU:0, one launch (start us, length us, event | category | flops | bytes accessed | tf_op | source)
XLA Modules:
  0.0 77.5 jit_solution(3104692198327845186)
XLA Ops:
  0.0 2.7 %pack.1 = (bf16[128,640]{1,0:T(8,128)(2,1)S(1)}, bf16[256,640]{1,0:T(8,128)(2,1)S(1)}, bf16[256,640]{1,0:T(8,128)(2,1)S(1)}, bf16[256,640]{1,0:T(8,128)(2,1)S(1)...) custom-call(s32[4,8]{1,0:T(4,128)} %ids.1, bf16[16,64,1280]{2,1,0:T(8,128)(2,1)} %keys.1, ...), custom_call_target="tpu_custom_call" | custom-call | bytes 12582912 | tf_op jit(solution)/shard_map/pack/pallas_call | solution.py:118
  2.7 0.5 collective-permute-start
  3.2 2.6 %collective-permute-start.5 = (bf16[1280,640]{1,0:T(8,128)(2,1)S(1)}, bf16[1280,640]{1,0:T(8,128)(2,1)S(1)}, u32[]{:S(2)}, u32[]{:S(2)}) collective-permute-start(bf16[1280,640]{1,0:T(8,128)(2,1)S(1)} %get-tuple-element.28), channel_id=1, source_target_pairs={{0,2},{2,0},{1,3},{3,1},{4,6},{6,4},{5,7},{7,5},{8,10},{10,8},{9,1... | collective-permute-start | bytes 4915208 | tf_op jit(solution)/shard_map/ppermute | solution.py:480
  5.8 2.6 %collective-permute-start.1 = (bf16[256,640]{1,0:T(8,128)(2,1)S(1)}, bf16[256,640]{1,0:T(8,128)(2,1)S(1)}, u32[]{:S(2)}, u32[]{:S(2)}) collective-permute-start(bf16[256,640]{1,0:T(8,128)(2,1)S(1)} %get-tuple-element.24), channel_id=1, source_target_pairs={{0,8},{4,12},{8,0},{12,4},{1,9},{5,13},{9,1},{13,5},{2,10},{6,14},... | collective-permute-start | bytes 983048 | tf_op jit(solution)/shard_map/ppermute | solution.py:479
  8.4 1.3 %collective-permute-start.2 = (bf16[256,640]{1,0:T(8,128)(2,1)S(1)}, bf16[256,640]{1,0:T(8,128)(2,1)S(1)}, u32[]{:S(2)}, u32[]{:S(2)}) collective-permute-start(bf16[256,640]{1,0:T(8,128)(2,1)S(1)} %get-tuple-element.25), channel_id=1, source_target_pairs={{0,12},{4,8},{8,4},{12,0},{1,13},{5,9},{9,5},{13,1},{2,14},{6,10},... | collective-permute-start | bytes 983048 | tf_op jit(solution)/shard_map/ppermute | solution.py:479
  10.0 11.3 %attend_current.1 = (f32[5,1024,128]{2,1,0:T(8,128)S(1)}, f32[5,1024,128]{2,1,0:T(8,128)S(1)}, bf16[1024,640]{1,0:T(8,128)(2,1)S(1)}) custom-call(bf16[1024,1280]{1,0:T(8,128)(2,1)} %queries.1, bf16[512,1280]{1,0:T(8,128)(2,1)} %own_keys.1, bf16[512,1280]{1,0:T(8,128)(2,1)} %own_values.1, bf16[1152,640]{1,0:T(8,128)(2,1)S(1)} %collective-permute-done.sibling.rest_0_.rest_4_), custom_call_target="tpu_custom_call" | custom-call | flops 4026531840 | bytes 7864320 | tf_op jit(solution)/shard_map/attend_current/pallas_call | solution.py:255
  21.3 3.6 %load.1 = (bf16[1280,2560]{1,0:T(8,128)(2,1)S(1)}, f32[8,64]{1,0:T(8,128)S(1)}) custom-call(s32[4,8]{1,0:T(4,128)} %ids.1, s32[128]{0:T(128)} %counts.1, bf16[1280,2560]{1,0:T(8,128)(2,1)} %weight.3, f32[5,1024,128]{2,1,0:T(8,128)S(1)} %get-tuple-element.19.after.lse), custom_call_target="tpu_custom_call" | custom-call | bytes 6553600 | tf_op jit(solution)/shard_map/load/pallas_call | solution.py:174
  24.9 6.4 %collective-permute-done.1.refs_0_.rest_1_ = bf16[256,640]{1,0:T(8,128)(2,1)S(1)} collective-permute-done((bf16[256,640]{1,0:T(8,128)(2,1)S(1)}, bf16[256,640]{1,0:T(8,128)(2,1)S(1)}, u32[]{:S(2)}, u32[]{:S(2)}) %collective-permute-start.1) | collective-permute-done | bytes 327712 | tf_op jit(solution)/shard_map/ppermute | solution.py:479
  31.3 0.5 collective-permute-done.3.refs_2_.rest_3_
  32.0 1.4 %far_first.1 = (f32[5,512,128]{2,1,0:T(8,128)S(1)}, f32[5,512,128]{2,1,0:T(8,128)S(1)}) custom-call(f32[8,64]{1,0:T(8,128)S(1)} %get-tuple-element.20.bias, bf16[1024,640]{1,0:T(8,128)(2,1)S(1)} %get-tuple-element.21.q, f32[5,1024,128]{2,1,0:T(8,128)S(1)} %get-tuple-element.22.held, f32[5,1024,128]{2,1,0:T(8,128)S(1)} %get-tuple-element.19.after.lse, ...), custom_call_target="tpu_custom_call" | custom-call | flops 1024 | bytes 1024 | tf_op jit(solution)/shard_map/far_first/pallas_call | solution.py:328
  33.9 1.4 %far_last.1.after.mine = bf16[512,640]{1,0:T(8,128)(2,1)S(1)} custom-call(f32[8,64]{1,0:T(8,128)S(1)} %get-tuple-element.20.bias, bf16[1024,640]{1,0:T(8,128)(2,1)S(1)} %get-tuple-element.21.q, f32[5,512,128]{2,1,0:T(8,128)S(1)} %get-tuple-element.29.held, f32[5,512,128]{2,1,0:T(8,128)S(1)} %get-tuple-element.30.lse, ...), custom_call_target="tpu_custom_call" | custom-call | flops 1024 | bytes 1024 | tf_op jit(solution)/shard_map/far_last/pallas_call | solution.py:328
  36.0 6.5 %collective-permute-done.5.array.refs_3_ = bf16[1280,640]{1,0:T(8,128)(2,1)S(1)} collective-permute-done((bf16[1280,640]{1,0:T(8,128)(2,1)S(1)}, bf16[1280,640]{1,0:T(8,128)(2,1)S(1)}, u32[]{:S(2)}, u32[]{:S(2)}) %collective-permute-start.5) | collective-permute-done | bytes 1638432 | tf_op jit(solution)/shard_map/ppermute | solution.py:480
  42.5 2.0 %collective-permute-start.12 = (bf16[1280,512]{1,0:T(8,128)(2,1)S(1)}, bf16[1280,512]{1,0:T(8,128)(2,1)S(1)}, u32[]{:S(2)}, u32[]{:S(2)}) collective-permute-start(bf16[1280,512]{1,0:T(8,128)(2,1)S(1)} %leading.1.rest_8_), channel_id=1, source_target_pairs={{0,16},{16,0},{1,17},{17,1},{2,18},{18,2},{3,19},{19,3},{4,20},{20... | collective-permute-start | bytes 3932168 | tf_op jit(solution)/shard_map/ppermute | solution.py:495
  44.6 1.1 %collective-permute-start.11 = (bf16[1280,512]{1,0:T(8,128)(2,1)S(1)}, bf16[1280,512]{1,0:T(8,128)(2,1)S(1)}, u32[]{:S(2)}, u32[]{:S(2)}) collective-permute-start(bf16[1280,512]{1,0:T(8,128)(2,1)S(1)} %leading.1.rest_8_), channel_id=1, source_target_pairs={{0,4},{4,0},{8,12},{12,8},{1,5},{5,1},{9,13},{13,9},{2,6},{6,2},{1... | collective-permute-start | bytes 3932168 | tf_op jit(solution)/shard_map/ppermute | solution.py:496
  45.7 2.1 %near.1.rest_0_.mine = bf16[512,640]{1,0:T(8,128)(2,1)S(1)} custom-call(f32[8,64]{1,0:T(8,128)S(1)} %get-tuple-element.20.bias, bf16[1024,640]{1,0:T(8,128)(2,1)S(1)} %get-tuple-element.21.q, f32[5,1024,128]{2,1,0:T(8,128)S(1)} %get-tuple-element.22.held, f32[5,1024,128]{2,1,0:T(8,128)S(1)} %get-tuple-element.19.after.lse, ...), custom_call_target="tpu_custom_call" | custom-call | flops 1024 | bytes 1024 | tf_op jit(solution)/shard_map/near/pallas_call | solution.py:328
  47.8 1.9 %project_unshared.1.refs_1_ = bf16[512,896]{1,0:T(8,128)(2,1)S(1)} custom-call(bf16[512,640]{1,0:T(8,128)(2,1)S(1)} %far_last.1.after.mine, bf16[512,640]{1,0:T(8,128)(2,1)S(1)} %collective-permute-done.8.other, bf16[1280,2560]{1,0:T(8,128)(2,1)S(1)} %get-tuple-element.27.refs_3_.weight, bf16[512,640]{1,0:T(8,128)(2,1)S(1)} %near.1.rest_0_.mine), custom_call_target="tpu_custom_call" | custom-call | flops 1024 | bytes 1024 | tf_op jit(solution)/shard_map/project_unshared/pallas_call | solution.py:378
  49.7 1.7 %collective-permute-start.9 = (bf16[512,896]{1,0:T(8,128)(2,1)S(1)}, bf16[512,896]{1,0:T(8,128)(2,1)S(1)}, u32[]{:S(2)}, u32[]{:S(2)}) collective-permute-start(bf16[512,896]{1,0:T(8,128)(2,1)S(1)} %project_unshared.1.refs_1_), channel_id=1, source_target_pairs={{0,2},{2,0},{1,3},{3,1},{4,6},{6,4},{5,7},{7,5},{8,10},{10,8},{9,1... | collective-permute-start | bytes 2752520 | tf_op jit(solution)/shard_map/ppermute | solution.py:502
  51.4 5.1 %collective-permute-done.7.refs_0_ = bf16[512,640]{1,0:T(8,128)(2,1)S(1)} collective-permute-done((bf16[512,640]{1,0:T(8,128)(2,1)S(1)}, bf16[512,640]{1,0:T(8,128)(2,1)S(1)}, u32[]{:S(2)}, u32[]{:S(2)}) %collective-permute-start.7) | collective-permute-done | bytes 655392 | tf_op jit(solution)/shard_map/ppermute | solution.py:492
  56.5 4.4 %project.1.refs_0_.terms = bf16[512,2560]{1,0:T(8,128)(2,1)S(1)} custom-call(bf16[512,640]{1,0:T(8,128)(2,1)S(1)} %near.1.rest_0_.mine, bf16[512,640]{1,0:T(8,128)(2,1)S(1)} %collective-permute-done.6.other, bf16[1280,2560]{1,0:T(8,128)(2,1)S(1)} %get-tuple-element.27.refs_3_.weight, bf16[512,640]{1,0:T(8,128)(2,1)S(1)} %gate.1.rest_0_.refs_1_.mine), custom_call_target="tpu_custom_call" | custom-call | flops 1024 | bytes 1024 | tf_op jit(solution)/shard_map/project/pallas_call | solution.py:378
  60.9 2.1 %add_remote.3.total = bf16[512,2560]{1,0:T(8,128)(2,1)} custom-call(bf16[512,2560]{1,0:T(8,128)(2,1)S(1)} %project.1.refs_0_.terms, bf16[512,640]{1,0:T(8,128)(2,1)S(1)} %gate.1.rest_0_.refs_1_.mine, bf16[512,640]{1,0:T(8,128)(2,1)S(1)} %collective-permute-done.10.refs_2_.other, bf16[1280,640]{1,0:T(8,128)(2,1)S(1)} %collective-permute-done.5.array.refs_3_), custom_call_target="tpu_custom_call" | custom-call | flops 1024 | bytes 1024 | tf_op jit(solution)/shard_map/add_remote/pallas_call | solution.py:442
  63.0 9.8 %collective-permute-done.12.weight = bf16[1280,512]{1,0:T(8,128)(2,1)S(1)} collective-permute-done((bf16[1280,512]{1,0:T(8,128)(2,1)S(1)}, bf16[1280,512]{1,0:T(8,128)(2,1)S(1)}, u32[]{:S(2)}, u32[]{:S(2)}) %collective-permute-start.12) | collective-permute-done | bytes 1310752 | tf_op jit(solution)/shard_map/ppermute | solution.py:495
  72.9 1.7 %add_remote.4.total = bf16[512,2560]{1,0:T(8,128)(2,1)} custom-call(bf16[512,2560]{1,0:T(8,128)(2,1)S(1)} %project.1.refs_0_.terms, bf16[512,640]{1,0:T(8,128)(2,1)S(1)} %gate.1.rest_0_.refs_1_.mine, bf16[512,640]{1,0:T(8,128)(2,1)S(1)} %collective-permute-done.10.refs_2_.other, ...), custom_call_target="tpu_custom_call", output_to_operand_aliasing={{}: (4, {})} | custom-call | flops 1024 | bytes 1024 | tf_op jit(solution)/shard_map/add_remote/pallas_call | solution.py:442
  74.6 1.7 %add_remote.5.total = bf16[512,2560]{1,0:T(8,128)(2,1)} custom-call(bf16[512,2560]{1,0:T(8,128)(2,1)S(1)} %project.1.refs_0_.terms, bf16[512,640]{1,0:T(8,128)(2,1)S(1)} %gate.1.rest_0_.refs_1_.mine, bf16[512,640]{1,0:T(8,128)(2,1)S(1)} %collective-permute-done.10.refs_2_.other, ...), custom_call_target="tpu_custom_call", output_to_operand_aliasing={{}: (4, {})} | custom-call | flops 1024 | bytes 1024 | tf_op jit(solution)/shard_map/add_remote/pallas_call | solution.py:442
  76.4 1.1 %add_unshared.1 = bf16[512,2560]{1,0:T(8,128)(2,1)} custom-call(bf16[512,2560]{1,0:T(8,128)(2,1)S(1)} %project.1.refs_0_.terms, bf16[512,896]{1,0:T(8,128)(2,1)S(1)} %collective-permute-done.9.came, bf16[512,2560]{1,0:T(8,128)(2,1)} %add_remote.5.total), custom_call_target="tpu_custom_call", output_to_operand_aliasing={{}: (2, {})} | custom-call | flops 1024 | bytes 1024 | tf_op jit(solution)/shard_map/add_unshared/pallas_call | solution.py:442
  (17 shorter events, 1.6 us)
Async XLA Ops:
  2.7 7.3 %collective-permute-start = (bf16[1152,640]{1,0:T(8,128)(2,1)S(1)}, bf16[1152,640]{1,0:T(8,128)(2,1)S(1)}, u32[]{:S(2)}, u32[]{:S(2)}) collective-permute-start(bf16[1152,640]{1,0:T(8,128)(2,1)S(1)} %get-tuple-element.18), channel_id=1, source_target_pairs={{0,1},{1,0},{2,3},{3,2},{4,5},{5,4},{6,7},{7,6},{8,9},{9,8},{10,11... | collective-permute-start | bytes 4423688 | tf_op jit(solution)/shard_map/ppermute | solution.py:481
  3.2 39.2 %collective-permute-start.5 = (bf16[1280,640]{1,0:T(8,128)(2,1)S(1)}, bf16[1280,640]{1,0:T(8,128)(2,1)S(1)}, u32[]{:S(2)}, u32[]{:S(2)}) collective-permute-start(bf16[1280,640]{1,0:T(8,128)(2,1)S(1)} %get-tuple-element.28), channel_id=1, source_target_pairs={{0,2},{2,0},{1,3},{3,1},{4,6},{6,4},{5,7},{7,5},{8,10},{10,8},{9,1... | collective-permute-start | bytes 4915208 | tf_op jit(solution)/shard_map/ppermute | solution.py:480
  5.8 25.5 %collective-permute-start.1 = (bf16[256,640]{1,0:T(8,128)(2,1)S(1)}, bf16[256,640]{1,0:T(8,128)(2,1)S(1)}, u32[]{:S(2)}, u32[]{:S(2)}) collective-permute-start(bf16[256,640]{1,0:T(8,128)(2,1)S(1)} %get-tuple-element.24), channel_id=1, source_target_pairs={{0,8},{4,12},{8,0},{12,4},{1,9},{5,13},{9,1},{13,5},{2,10},{6,14},... | collective-permute-start | bytes 983048 | tf_op jit(solution)/shard_map/ppermute | solution.py:479
  8.4 23.0 %collective-permute-start.2 = (bf16[256,640]{1,0:T(8,128)(2,1)S(1)}, bf16[256,640]{1,0:T(8,128)(2,1)S(1)}, u32[]{:S(2)}, u32[]{:S(2)}) collective-permute-start(bf16[256,640]{1,0:T(8,128)(2,1)S(1)} %get-tuple-element.25), channel_id=1, source_target_pairs={{0,12},{4,8},{8,4},{12,0},{1,13},{5,9},{9,5},{13,1},{2,14},{6,10},... | collective-permute-start | bytes 983048 | tf_op jit(solution)/shard_map/ppermute | solution.py:479
  9.7 22.2 %collective-permute-start.3 = (bf16[256,640]{1,0:T(8,128)(2,1)S(1)}, bf16[256,640]{1,0:T(8,128)(2,1)S(1)}, u32[]{:S(2)}, u32[]{:S(2)}) collective-permute-start(bf16[256,640]{1,0:T(8,128)(2,1)S(1)} %get-tuple-element.26), channel_id=1, source_target_pairs={{0,4},{4,0},{8,12},{12,8},{1,5},{5,1},{9,13},{13,9},{2,6},{6,2},{1... | collective-permute-start | bytes 983048 | tf_op jit(solution)/shard_map/ppermute | solution.py:479
  31.9 1.9 %collective-permute-start.4 = (bf16[384,640]{1,0:T(8,128)(2,1)S(1)}, bf16[384,640]{1,0:T(8,128)(2,1)S(1)}, u32[]{:S(2)}, u32[]{:S(2)}) collective-permute-start(bf16[384,640]{1,0:T(8,128)(2,1)S(1)} %pass_on.1.rest_4_), channel_id=1, source_target_pairs={{0,1},{1,0},{2,3},{3,2},{4,5},{5,4},{6,7},{7,6},{8,9},{9,8},{10,11... | collective-permute-start | bytes 1474568 | tf_op jit(solution)/shard_map/ppermute | solution.py:486
  35.2 12.5 %collective-permute-start.8 = (bf16[512,640]{1,0:T(8,128)(2,1)S(1)}, bf16[512,640]{1,0:T(8,128)(2,1)S(1)}, u32[]{:S(2)}, u32[]{:S(2)}) collective-permute-start(bf16[512,640]{1,0:T(8,128)(2,1)S(1)} %far_last.1.after.mine), channel_id=1, source_target_pairs={{0,1},{1,0},{2,3},{3,2},{4,5},{5,4},{6,7},{7,6},{8,9},{9,8},{10,11... | collective-permute-start | bytes 1966088 | tf_op jit(solution)/shard_map/ppermute | solution.py:493
  35.5 21.0 %collective-permute-start.7 = (bf16[512,640]{1,0:T(8,128)(2,1)S(1)}, bf16[512,640]{1,0:T(8,128)(2,1)S(1)}, u32[]{:S(2)}, u32[]{:S(2)}) collective-permute-start(bf16[512,640]{1,0:T(8,128)(2,1)S(1)} %far_last.1.after.mine), channel_id=1, source_target_pairs={{0,2},{2,0},{1,3},{3,1},{4,6},{6,4},{5,7},{7,5},{8,10},{10,8},{9,1... | collective-permute-start | bytes 1966088 | tf_op jit(solution)/shard_map/ppermute | solution.py:492
  42.5 30.3 %collective-permute-start.12 = (bf16[1280,512]{1,0:T(8,128)(2,1)S(1)}, bf16[1280,512]{1,0:T(8,128)(2,1)S(1)}, u32[]{:S(2)}, u32[]{:S(2)}) collective-permute-start(bf16[1280,512]{1,0:T(8,128)(2,1)S(1)} %leading.1.rest_8_), channel_id=1, source_target_pairs={{0,16},{16,0},{1,17},{17,1},{2,18},{18,2},{3,19},{19,3},{4,20},{20... | collective-permute-start | bytes 3932168 | tf_op jit(solution)/shard_map/ppermute | solution.py:495
  44.6 30.0 %collective-permute-start.11 = (bf16[1280,512]{1,0:T(8,128)(2,1)S(1)}, bf16[1280,512]{1,0:T(8,128)(2,1)S(1)}, u32[]{:S(2)}, u32[]{:S(2)}) collective-permute-start(bf16[1280,512]{1,0:T(8,128)(2,1)S(1)} %leading.1.rest_8_), channel_id=1, source_target_pairs={{0,4},{4,0},{8,12},{12,8},{1,5},{5,1},{9,13},{13,9},{2,6},{6,2},{1... | collective-permute-start | bytes 3932168 | tf_op jit(solution)/shard_map/ppermute | solution.py:496
  49.7 26.6 %collective-permute-start.9 = (bf16[512,896]{1,0:T(8,128)(2,1)S(1)}, bf16[512,896]{1,0:T(8,128)(2,1)S(1)}, u32[]{:S(2)}, u32[]{:S(2)}) collective-permute-start(bf16[512,896]{1,0:T(8,128)(2,1)S(1)} %project_unshared.1.refs_1_), channel_id=1, source_target_pairs={{0,2},{2,0},{1,3},{3,1},{4,6},{6,4},{5,7},{7,5},{8,10},{10,8},{9,1... | collective-permute-start | bytes 2752520 | tf_op jit(solution)/shard_map/ppermute | solution.py:502
  51.4 5.1 %collective-permute-start.6 = (bf16[512,640]{1,0:T(8,128)(2,1)S(1)}, bf16[512,640]{1,0:T(8,128)(2,1)S(1)}, u32[]{:S(2)}, u32[]{:S(2)}) collective-permute-start(bf16[512,640]{1,0:T(8,128)(2,1)S(1)} %near.1.rest_0_.mine), channel_id=1, source_target_pairs={{0,1},{1,0},{2,3},{3,2},{4,5},{5,4},{6,7},{7,6},{8,9},{9,8},{10,11... | collective-permute-start | bytes 1966088 | tf_op jit(solution)/shard_map/ppermute | solution.py:499
  56.5 4.4 %collective-permute-start.10 = (bf16[512,640]{1,0:T(8,128)(2,1)S(1)}, bf16[512,640]{1,0:T(8,128)(2,1)S(1)}, u32[]{:S(2)}, u32[]{:S(2)}) collective-permute-start(bf16[512,640]{1,0:T(8,128)(2,1)S(1)} %gate.1.rest_0_.refs_1_.mine), channel_id=1, source_target_pairs={{0,1},{1,0},{2,3},{3,2},{4,5},{5,4},{6,7},{7,6},{8,9},{9,8},{10,11... | collective-permute-start | bytes 1966088 | tf_op jit(solution)/shard_map/ppermute | solution.py:504
